TPU v7x, 128 devices: a whole 4x4x4 slice. The times are simulated.
128 devices in a mesh: section: 2 (over core), row: 4 (over y), col: 16 (over x, z).
Axes of the slice: x: 4, y: 4, z: 4, core: 2. Of those that a mesh axis runs over, the one named last changes fastest.
Arguments:
- images: bfloat16 [2, 128, 50, 768], P(None, ('row', 'col')), may hold values from -6 to 6
- cotangent: bfloat16 [2, 128, 50, 768], P(None, ('row', 'col')), may hold values from -6 to 6
- norm_gains: bfloat16 [2, 2, 768], P('section', None, ('row', 'col')), may hold values from 0.25 to 1.75
- attn_qkv: bfloat16 [2, 768, 3, 768], P('section', 'col', None, 'row'), may hold values from -0.21875 to 0.21875
- attn_out: bfloat16 [2, 768, 768], P('section', 'row', 'col'), may hold values from -0.875 to 0.875
- router: bfloat16 [2, 768, 32], P('section', ('row', 'col')), may hold values from -0.15625 to 0.15625
- expert_in: bfloat16 [2, 768, 98304], P('section', None, ('row', 'col')), may hold values from -0.21875 to 0.21875
- expert_out: bfloat16 [2, 98304, 768], P('section', ('row', 'col')), may hold values from -1.75 to 1.75
- routes: int32 [2, 2, 128, 50, 2], P('section', None, ('row', 'col')), may hold values from 0 to 31, all different within a row; in each aligned block of 100 rows (0 to 99, 100 to 199, ..., all dimensions but the last counted through in order) at most 8 rows name the same one
Outputs:
- section_out: bfloat16 [2, 2, 128, 50, 768], P('section', None, ('row', 'col'))
- input_grads: float32 [2, 2, 128, 50, 768], P('section', None, ('row', 'col'))
- grad_gains: float32 [2, 2, 768], P('section', None, ('row', 'col'))
- grad_qkv: float32 [2, 768, 3, 768], P('section', 'col', None, 'row')
- grad_attn_out: float32 [2, 768, 768], P('section', 'row', 'col')
- grad_router: float32 [2, 768, 32], P('section', ('row', 'col'))
- grad_expert_in: float32 [2, 768, 98304], P('section', None, ('row', 'col'))
- grad_expert_out: float32 [2, 98304, 768], P('section', ('row', 'col'))
Inputs may be any that keep to these rules, and one draw needn't show every extreme that they name: `routes`: each token names two different experts; among the tokens of one device of one section and micro-batch (aligned blocks of 100 tokens) no expert is named more than 8 times, a bound that some block reaches.
All inputs are finite; a program needn't handle non-finite values.
Results may differ from a plain program's by a relative error of at most 0.03.
Values may be sent and summed in bfloat16 or wider, within the bound.
No kernel may reach another device: no remote copies, remote signals or barrier semaphores. Data moves between devices by JAX's collectives and lax.ppermute only.
A program may use at most 192 MiB of HBM per device.

v0:
```python
import functools

import jax
import jax.numpy as jnp
from jax import lax
from jax.experimental import pallas as pl
from jax.experimental.pallas import tpu as pltpu
from jax.sharding import PartitionSpec as P

HEAD = 64
WIDTH = 768
SEQ = 50
SPAN = 56
PAD = 2 * SPAN
EXPERTS = 32
SLOTS = 8
ROWS = 4
COLS = 16
CHIPS = ROWS * COLS
PART = WIDTH // COLS
SMALL = WIDTH // CHIPS
FILL = CHIPS * SLOTS
HIDDEN = 1536
STEP = 512
EPSILON = 1e-06
SCALE = float(HEAD) ** (-0.5)
VMEM = 58 * 1024 * 1024
BF = jnp.bfloat16
F32 = jnp.float32


def dot(left, right):
    return jnp.dot(left, right, preferred_element_type=F32)


def dot_tn(left, right):
    return lax.dot_general(left, right, (((0,), (0,)), ((), ())), preferred_element_type=F32)


def dot_nt(left, right):
    return lax.dot_general(left, right, (((1,), (1,)), ((), ())), preferred_element_type=F32)


def iota(shape, axis):
    return lax.broadcasted_iota(jnp.int32, shape, axis)


def hot(flag):
    return jnp.where(flag, 1.0, 0.0)


def normalise(values):
    centred = values - jnp.mean(values, axis=-1, keepdims=True)
    spread = jnp.mean(centred * centred, axis=-1, keepdims=True)
    inverse = lax.rsqrt(spread + EPSILON)
    return centred * inverse, inverse


def normalise_back(grad, unit, inverse):
    return inverse * (
        grad
        - jnp.mean(grad, axis=-1, keepdims=True)
        - unit * jnp.mean(grad * unit, axis=-1, keepdims=True)
    )


def gelu_parts(values):
    bell = jnp.exp(-0.5 * values * values)
    t = 1.0 / (1.0 + (0.3275911 * 0.7071067811865476) * jnp.abs(values))
    poly = 1.061405429 * t - 1.453152027
    poly = poly * t + 1.421413741
    poly = poly * t - 0.284496736
    poly = poly * t + 0.254829592
    tail = (0.5 * t) * poly * bell
    below = jnp.where(values < 0, tail, 1.0 - tail)
    return values * below, below + values * (0.3989422804014327 * bell)


def half_turn(values):
    return pltpu.roll(values, HEAD, 1)


def lane_low(rows):
    return iota((rows, 2 * HEAD), 1) < HEAD


def weight_reader(core, own_ref, other_ref, w_ref, small_ref, sems):
    small_copy = pltpu.make_async_copy(own_ref.at[:, 3 * PART : 3 * PART + 16, :], small_ref, sems.at[6, 0])
    small_copy.start()

    def copy(ref, half, r, b):
        at = (3 * half + b) * 128
        return pltpu.make_async_copy(
            ref.at[r * COLS : (r + 1) * COLS, b * PART : (b + 1) * PART, :],
            w_ref.at[r, :, :, at : at + 128],
            sems.at[3 * half + b, r],
        )

    def start(refs):
        for r in range(ROWS):
            for half in range(2):
                for b in range(3):
                    copy(refs[half], half, r, b).start()

    @pl.when(core == 0)
    def _():
        start((own_ref, other_ref))

    @pl.when(core == 1)
    def _():
        start((other_ref, own_ref))

    def wait():
        for r in range(ROWS):
            for half in range(2):
                for b in range(3):
                    copy(own_ref, half, r, b).wait()

    def read(r, first, last):
        return w_ref[r, :, :, first:last].reshape(WIDTH, last - first)

    return small_copy.wait, wait, read


def small_places():
    shape = (COLS * SMALL, COLS * 16)
    inside = iota(shape, 1)
    place = jnp.bitwise_and(inside, 15)
    wanted = lax.shift_right_logical(inside, 4) * SMALL + place
    return hot((iota(shape, 0) == wanted) & (place < SMALL)).astype(BF)


def unpack_small(small_ref):
    packed = small_ref[...].reshape(ROWS, COLS * 16, 128)
    places = small_places()
    small = jnp.concatenate([dot(places, packed[r]) for r in range(ROWS)], axis=0).astype(BF)
    pick = hot(iota((8, 128), 1) == iota((8, 128), 0) + EXPERTS).astype(BF)
    gains = dot_nt(pick, small)
    return small, gains[0:1], gains[1:2]


def routing(core, section, own_ref, other_ref):
    chosen = jnp.where(core == section, own_ref[core], other_ref[core])
    first = chosen[:, 0:1]
    second = chosen[:, 1:2]
    lane = iota((PAD, 128), 1)
    hot0 = hot(lane == first)
    hot1 = hot(lane == second)
    before = hot(iota((PAD, PAD), 0) > iota((PAD, PAD), 1)).astype(BF)
    earlier = dot(before, (hot0 + hot1).astype(BF))
    place = iota((PAD, FILL), 1)

    def spread(expert, marks):
        slot = jnp.sum(earlier * marks, axis=1, keepdims=True).astype(jnp.int32)
        base = expert * (2 * SLOTS) + slot
        return hot((place == base) | (place == base + SLOTS)).astype(BF)

    return hot0, hot1, spread(first, hot0), spread(second, hot1)


def gates(chance, marks):
    return jnp.sum(chance * marks, axis=1, keepdims=True)


def image_bias():
    query = iota((PAD, PAD), 0)
    key = iota((PAD, PAD), 1)
    first = (query < SPAN) & (key < SEQ)
    second = (query >= SPAN) & (key >= SPAN) & (key < SPAN + SEQ)
    bias = jnp.where(first | second, 0.0, -1e30)
    return jnp.concatenate([bias] * 3, axis=0)


def read_tokens(ref):
    blank = jnp.zeros((SPAN - SEQ, WIDTH), F32)
    return jnp.concatenate([ref[0].astype(F32), blank, ref[1].astype(F32), blank], axis=0)


def write_tokens(ref, values):
    ref[0] = values[:SEQ].astype(ref.dtype)
    ref[1] = values[SPAN : SPAN + SEQ].astype(ref.dtype)


def attention_forward(x, wait, read, gain, m_ref, p_ref, o_ref):
    unit, _ = normalise(x)
    a = (unit * gain).astype(BF)
    low = lane_low(PAD)
    low_b = hot(low).astype(BF)
    high_b = (1.0 - hot(low)).astype(BF)
    bias = image_bias()
    branch = jnp.zeros((PAD, WIDTH), F32)
    wait()
    for r in range(ROWS):
        wide = dot(a, read(r, 0, 512))
        m5 = dot(a, read(r, 640, 768)).astype(BF)
        m = wide.astype(BF)
        m_ref[:, r * 640 : r * 640 + 512] = m
        m_ref[:, r * 640 + 512 : r * 640 + 640] = m5
        q, k, v, qk = m[:, 0:128], m[:, 128:256], m[:, 256:384], m[:, 384:512]
        k2 = half_turn(wide[:, 384:512]).astype(BF)
        qs = jnp.concatenate([q * low_b, q * high_b], axis=0)
        s = jnp.concatenate([dot_nt(qs, k), dot_nt(qk * low_b, k2)], axis=0)
        s = s * SCALE + bias
        e = jnp.exp(s - jnp.max(s, axis=-1, keepdims=True))
        p = (e / jnp.sum(e, axis=-1, keepdims=True)).astype(BF)
        p_ref[r * 3 * PAD : (r + 1) * 3 * PAD, :] = p
        os = dot(p[: 2 * PAD], v)
        o2 = dot(p[2 * PAD :], m5)
        o01 = jnp.where(low, os[:PAD], os[PAD:])
        o2 = jnp.where(low, 0.0, half_turn(o2))
        o = jnp.concatenate([o01, o2], axis=1).astype(BF)
        o_ref[:, r * 256 : (r + 1) * 256] = o
        branch = branch + dot_nt(o, read(r, 512, 768))
    return x + branch


def route_forward(h, small, gain):
    unit, _ = normalise(h)
    b = (unit * gain).astype(BF)
    logits = dot(b, small)
    inside = iota((PAD, 128), 1) < EXPERTS
    logits = jnp.where(inside, logits, -1e30)
    e = jnp.exp(logits - jnp.max(logits, axis=-1, keepdims=True))
    e = jnp.where(inside, e, 0.0)
    return b, e / jnp.sum(e, axis=-1, keepdims=True)


def attention_backward(dh, x, gain, wait, read, m_ref, p_ref, o_ref, take):
    db = dh.astype(BF)
    unit, inverse = normalise(x)
    a = (unit * gain).astype(BF)
    low = lane_low(PAD)
    low_b = hot(low).astype(BF)
    high_b = (1.0 - hot(low)).astype(BF)
    da = jnp.zeros((PAD, WIDTH), F32)
    wait()
    for r in range(ROWS):
        o = o_ref[:, r * 256 : (r + 1) * 256]
        q = m_ref[:, r * 640 : r * 640 + 128]
        k = m_ref[:, r * 640 + 128 : r * 640 + 256]
        v = m_ref[:, r * 640 + 256 : r * 640 + 384]
        qk = m_ref[:, r * 640 + 384 : r * 640 + 512]
        m5 = m_ref[:, r * 640 + 512 : r * 640 + 640]
        k2 = half_turn(qk.astype(F32)).astype(BF)
        q2 = qk * low_b
        qs = jnp.concatenate([q * low_b, q * high_b], axis=0)
        pb = p_ref[r * 3 * PAD : (r + 1) * 3 * PAD, :]
        p = pb.astype(F32)
        do = dot(db, read(r, 512, 768))
        do01 = do[:, 0:128].astype(BF)
        do2 = half_turn(do[:, 128:256]).astype(BF) * low_b
        dos = jnp.concatenate([do01 * low_b, do01 * high_b], axis=0)
        dp = jnp.concatenate([dot_nt(dos, v), dot_nt(do2, m5)], axis=0)
        ds = (p * (dp - jnp.sum(dp * p, axis=-1, keepdims=True))).astype(BF)
        dv = dot_tn(pb[: 2 * PAD], dos)
        dv2 = dot_tn(pb[2 * PAD :], do2)
        dqs = dot(ds[: 2 * PAD], k)
        dq = jnp.where(low, dqs[:PAD], dqs[PAD:]) * SCALE
        dk = dot_tn(ds[: 2 * PAD], qs) * SCALE
        dq2 = dot(ds[2 * PAD :], k2) * SCALE
        dk2 = dot_tn(ds[2 * PAD :], q2) * SCALE
        dqk = jnp.where(low, dq2, half_turn(dk2))
        dm = jnp.concatenate([dq, dk, dv, dqk, dv2], axis=1).astype(BF)
        da = da + dot_nt(dm[:, :512], read(r, 0, 512)) + dot_nt(dm[:, 512:], read(r, 640, 768))
        take(r, a, db, dm)
    dx = dh + normalise_back(da * gain, unit, inverse)
    return dx, a, db, (da * unit).astype(BF)


def projection_grads(r, a, db, dm, o, g_ref):
    gm = dot_tn(a, dm)
    go = dot_tn(db, o)
    blocks = [gm[:, i * 128 : (i + 1) * 128] for i in range(4)]
    blocks += [go[:, :128], gm[:, 512:640] + go[:, 128:256]]
    for i, block in enumerate(blocks):
        at = i % 3 * PART
        g_ref[i // 3, r * COLS : (r + 1) * COLS, at : at + PART, :] = block.astype(BF).reshape(
            COLS, PART, 128
        )


def small_grads(b, dl, terms1, terms2, g_ref):
    lane = iota((PAD, 128), 1)
    gs = dot_tn(b, dl)
    gs = gs + dot_tn(terms1, hot(lane == EXPERTS).astype(BF))
    gs = gs + dot_tn(terms2, hot(lane == EXPERTS + 1).astype(BF))
    gs = gs.astype(BF).reshape(ROWS, COLS * SMALL, 128)
    places = small_places()
    spread = jnp.concatenate([dot_tn(places, gs[r]) for r in range(ROWS)], axis=0).astype(BF)
    spread = spread.reshape(CHIPS, 16, 128)
    g_ref[0, :, 3 * PART :, :] = spread
    g_ref[1, :, 3 * PART :, :] = spread


def layer_backward(dz, dr, marks, dgv, x, h, chance, small, gain1, gain2, wait, read, m_ref, p_ref, o_ref, take):
    _, _, d0, d1 = marks
    dn = dot(d0, dr).astype(BF).astype(F32) + dot(d1, dr).astype(BF).astype(F32)
    dl = (chance * (dgv - jnp.sum(dgv * chance, axis=1, keepdims=True))).astype(BF)
    dn = dn + dot_nt(dl, small)
    unit, inverse = normalise(h)
    dh = dz + normalise_back(dn * gain2, unit, inverse)
    dx, a, db, terms1 = attention_backward(dh, x, gain1, wait, read, m_ref, p_ref, o_ref, take)
    return dx, (a, db, dl, terms1, (dn * unit).astype(BF))


def ship(core, g_ref, keep_ref, send_ref, sems):
    copies = send([
        (g_ref.at[1 - core], send_ref, sems.at[0]),
        (g_ref.at[core], keep_ref, sems.at[1]),
    ])
    for copy in copies:
        copy.wait()


def gate_grads(dz, y_both, marks):
    hot0, hot1 = marks[0], marks[1]
    dg0 = jnp.sum(dz * y_both[:, :WIDTH].astype(F32), axis=1, keepdims=True)
    dg1 = jnp.sum(dz * y_both[:, WIDTH:].astype(F32), axis=1, keepdims=True)
    return dg0 * hot0 + dg1 * hot1


def grad_rows(dz, chance, marks):
    hot0, hot1, d0, d1 = marks
    dy0 = (gates(chance, hot0) * dz).astype(BF)
    dy1 = (gates(chance, hot1) * dz).astype(BF)
    return (dot_tn(d0, dy0) + dot_tn(d1, dy1)).astype(BF)


def combine(h, returned, chance, marks):
    hot0, hot1, d0, d1 = marks
    y0 = dot(d0, returned).astype(BF)
    y1 = dot(d1, returned).astype(BF)
    z = h + gates(chance, hot0) * y0.astype(F32) + gates(chance, hot1) * y1.astype(F32)
    return z, jnp.concatenate([y0, y1], axis=1)


def first_kernel(core_ref, x_ref, routes_ref, routes_other_ref, own_ref, other_ref, buf_ref, m_ref, p_ref, o_ref, h_ref, b_ref, c_ref, w_ref, small_ref, w_sems):
    core = core_ref[0]
    ready, wait, read = weight_reader(core, own_ref, other_ref, w_ref, small_ref, w_sems)
    ready()
    small, gain1, gain2 = unpack_small(small_ref)
    marks = routing(core, 0, routes_ref, routes_other_ref)
    h = attention_forward(read_tokens(x_ref.at[core]), wait, read, gain1, m_ref, p_ref, o_ref)
    b, chance = route_forward(h, small, gain2)
    h_ref[...] = h
    b_ref[...] = b
    c_ref[...] = chance
    buf_ref[...] = dot_tn(marks[2] + marks[3], b).astype(BF)


def middle_kernel(core_ref, back_ref, h0_ref, c0_ref, routes_ref, routes_other_ref, cot_ref, own_ref, other_ref, x_ref, y_ref, buf_ref, m_ref, p_ref, o_ref, h_ref, b_ref, c_ref, w_ref, small_ref, w_sems):
    core = core_ref[0]
    ready, wait, read = weight_reader(core, own_ref, other_ref, w_ref, small_ref, w_sems)
    marks = routing(core, 0, routes_ref, routes_other_ref)
    z, y_both = combine(h0_ref[...], back_ref[...], c0_ref[...], marks)
    write_tokens(x_ref, z)
    y_ref[...] = y_both
    ready()
    small, gain1, gain2 = unpack_small(small_ref)
    marks = routing(core, 1, routes_ref, routes_other_ref)
    x = read_tokens(x_ref)
    h = attention_forward(x, wait, read, gain1, m_ref, p_ref, o_ref)
    b, chance = route_forward(h, small, gain2)
    h_ref[...] = h
    b_ref[...] = b
    c_ref[...] = chance
    buf_ref[:, :WIDTH] = dot_tn(marks[2] + marks[3], b).astype(BF)
    buf_ref[:, WIDTH:] = grad_rows(read_tokens(cot_ref.at[core]), chance, marks)


def turn_kernel(core_ref, back_ref, routes_ref, routes_other_ref, cot_ref, x_ref, m_ref, p_ref, o_ref, h_ref, b_ref, c_ref, y0_ref, c0_ref, own_ref, other_ref, keep_ref, send_ref, dx_ref, gk_ref, gs_ref, buf_ref, dgv_ref, w_ref, small_ref, w_sems, g_ref, sems):
    core = core_ref[0]
    ready, wait, read = weight_reader(core, own_ref, other_ref, w_ref, small_ref, w_sems)
    ready()
    small, gain1, gain2 = unpack_small(small_ref)
    marks = routing(core, 1, routes_ref, routes_other_ref)
    chance = c_ref[...]
    h = h_ref[...]
    z, y_both = combine(h, back_ref[:, :WIDTH], chance, marks)
    x = read_tokens(x_ref)
    on_first = core == 0
    write_tokens(keep_ref, jnp.where(on_first, x, z))
    write_tokens(send_ref, jnp.where(on_first, z, x))
    dz = read_tokens(cot_ref.at[core])
    dgv = gate_grads(dz, y_both, marks)

    def take(r, a, db, dm):
        projection_grads(r, a, db, dm, o_ref[:, r * 256 : (r + 1) * 256], g_ref)

    dx, terms = layer_backward(dz, back_ref[:, WIDTH:], marks, dgv, x, h, chance, small, gain1, gain2, wait, read, m_ref, p_ref, o_ref, take)
    dx_ref[...] = dx
    small_grads(b_ref[...], *terms[2:], g_ref)
    dz = dx.astype(BF).astype(F32)
    marks = routing(core, 0, routes_ref, routes_other_ref)
    buf_ref[...] = grad_rows(dz, c0_ref[...], marks)
    dgv_ref[...] = gate_grads(dz, y0_ref[...], marks)
    ship(core, g_ref, gk_ref, gs_ref, sems)


def last_kernel(core_ref, back_ref, routes_ref, routes_other_ref, dz_ref, dgv_ref, x_ref, m_ref, p_ref, o_ref, h_ref, b_ref, c_ref, own_ref, other_ref, keep_ref, send_ref, gk_ref, gs_ref, w_ref, small_ref, w_sems, g_ref, sems):
    core = core_ref[0]
    ready, wait, read = weight_reader(core, own_ref, other_ref, w_ref, small_ref, w_sems)
    ready()
    small, gain1, gain2 = unpack_small(small_ref)
    marks = routing(core, 0, routes_ref, routes_other_ref)
    dx1 = dz_ref[...]
    dz = dx1.astype(BF).astype(F32)

    def take(r, a, db, dm):
        projection_grads(r, a, db, dm, o_ref[:, r * 256 : (r + 1) * 256], g_ref)

    dx, terms = layer_backward(dz, back_ref[...], marks, dgv_ref[...], read_tokens(x_ref.at[core]), h_ref[...], c_ref[...], small, gain1, gain2, wait, read, m_ref, p_ref, o_ref, take)
    small_grads(b_ref[...], *terms[2:], g_ref)
    on_first = core == 0
    write_tokens(keep_ref, jnp.where(on_first, dx, dx1))
    write_tokens(send_ref, jnp.where(on_first, dx1, dx))
    ship(core, g_ref, gk_ref, gs_ref, sems)


def whole_call(kernel, name, outs, args, weights):
    vmem = pl.BlockSpec(memory_space=pltpu.VMEM)
    far = pl.BlockSpec(memory_space=pl.ANY)
    scratch = [
        pltpu.VMEM((ROWS, COLS, PART, WIDTH), BF),
        pltpu.VMEM((CHIPS, 16, 128), BF),
        pltpu.SemaphoreType.DMA((7, ROWS)),
    ]
    if GRADS in outs:
        scratch += [pltpu.VMEM((2,) + GRADS[0], BF), pltpu.SemaphoreType.DMA((2,))]
    return pl.pallas_call(
        kernel,
        name=name,
        out_shape=[jax.ShapeDtypeStruct(shape, dtype) for shape, dtype in outs],
        in_specs=[pl.BlockSpec(memory_space=pltpu.SMEM)] + [vmem] * (len(args) - 1) + [far] * len(weights),
        out_specs=[far if out == GRADS else vmem for out in outs],
        scratch_shapes=scratch,
        compiler_params=pltpu.CompilerParams(vmem_limit_bytes=VMEM),
    )(*args, *weights)


SAVED = [
    ((PAD, ROWS * 640), BF),
    ((ROWS * 3 * PAD, PAD), BF),
    ((PAD, ROWS * 256), BF),
    ((PAD, WIDTH), F32),
    ((PAD, WIDTH), BF),
    ((PAD, 128), F32),
]
GRADS = ((CHIPS, 3 * PART + 16, 128), BF)


def fetch(core, section, own_refs, other_refs, places, sems):
    def start(refs):
        for j in range(HIDDEN // STEP):
            here = slice(j * STEP, (j + 1) * STEP)
            pltpu.make_async_copy(refs[0].at[:, here], places[0].at[:, here], sems.at[0, j]).start()
            pltpu.make_async_copy(refs[1].at[here, :], places[1].at[here, :], sems.at[1, j]).start()

    @pl.when(core == section)
    def _():
        start(own_refs)

    @pl.when(core != section)
    def _():
        start(other_refs)


def fetched(own_refs, places, sems, j):
    here = slice(j * STEP, (j + 1) * STEP)
    pltpu.make_async_copy(own_refs[0].at[:, here], places[0].at[:, here], sems.at[0, j]).wait()
    pltpu.make_async_copy(own_refs[1].at[here, :], places[1].at[here, :], sems.at[1, j]).wait()


def add_to(total, j, value):
    total[...] = value if j == 0 else total[...] + value


def send(pairs):
    copies = [pltpu.make_async_copy(*pair) for pair in pairs]
    for copy in copies:
        copy.start()
    return copies


def expert_forward_kernel(section, core_ref, rows_ref, a_ref, b_ref, c_ref, d_ref, y_ref, q_ref, gp_ref, w1, w2, sems, total, q_s, gp_s, out_sems):
    fetch(core_ref[0], section, (a_ref, c_ref), (b_ref, d_ref), (w1, w2), sems)
    copies = []
    for j in range(HIDDEN // STEP):
        fetched((a_ref, c_ref), (w1, w2), sems, j)
        here = slice(j * STEP, (j + 1) * STEP)
        q, gp = gelu_parts(dot(rows_ref[...], w1[:, here]))
        q = q.astype(BF)
        q_s[:, here] = q
        gp_s[:, here] = gp.astype(BF)
        add_to(total, j, dot(q, w2[here, :]))
        copies += send([
            (q_s.at[:, here], q_ref.at[:, here], out_sems.at[0, j]),
            (gp_s.at[:, here], gp_ref.at[:, here], out_sems.at[1, j]),
        ])
    y_ref[...] = total[...].astype(BF)
    for copy in copies:
        copy.wait()


def expert_both_kernel(section, core_ref, rows_ref, a_ref, b_ref, c_ref, d_ref, back_ref, q_ref, df_ref, w1, w2, sems, total, total_back, q_s, df_s, out_sems):
    fetch(core_ref[0], section, (a_ref, c_ref), (b_ref, d_ref), (w1, w2), sems)
    copies = []
    for j in range(HIDDEN // STEP):
        fetched((a_ref, c_ref), (w1, w2), sems, j)
        here = slice(j * STEP, (j + 1) * STEP)
        q, gp = gelu_parts(dot(rows_ref[:, :WIDTH], w1[:, here]))
        q = q.astype(BF)
        q_s[:, here] = q
        df = (dot_nt(rows_ref[:, WIDTH:], w2[here, :]) * gp).astype(BF)
        df_s[:, here] = df
        add_to(total, j, dot(q, w2[here, :]))
        add_to(total_back, j, dot_nt(df, w1[:, here]))
        copies += send([
            (q_s.at[:, here], q_ref.at[:, here], out_sems.at[0, j]),
            (df_s.at[:, here], df_ref.at[:, here], out_sems.at[1, j]),
        ])
    back_ref[:, :WIDTH] = total[...].astype(BF)
    back_ref[:, WIDTH:] = total_back[...].astype(BF)
    for copy in copies:
        copy.wait()


def expert_backward_kernel(section, core_ref, dy_ref, a_ref, b_ref, c_ref, d_ref, gp_far, back_ref, df_ref, w1, w2, sems, total, df_s, out_sems, gp_ref, in_sems):
    fetch(core_ref[0], section, (a_ref, c_ref), (b_ref, d_ref), (w1, w2), sems)
    kept = []
    for j in range(HIDDEN // STEP):
        here = slice(j * STEP, (j + 1) * STEP)
        kept += send([(gp_far.at[:, here], gp_ref.at[:, here], in_sems.at[0, j])])
    copies = []
    for j in range(HIDDEN // STEP):
        here = slice(j * STEP, (j + 1) * STEP)
        fetched((a_ref, c_ref), (w1, w2), sems, j)
        kept[j].wait()
        df = (dot_nt(dy_ref[...], w2[here, :]) * gp_ref[:, here].astype(F32)).astype(BF)
        df_s[:, here] = df
        add_to(total, j, dot_nt(df, w1[:, here]))
        copies += send([(df_s.at[:, here], df_ref.at[:, here], out_sems.at[0, j])])
    back_ref[...] = total[...].astype(BF)
    for copy in copies:
        copy.wait()


def expert_grads_kernel(rows_ref, dy_ref, q_ref, df_ref, g1_ref, g2_ref, turned):
    @pl.when(pl.program_id(0) == 0)
    def _():
        turned[...] = rows_ref[...].T

    g1_ref[...] = dot(turned[...], df_ref[...]).astype(BF)
    g2_ref[...] = dot_tn(q_ref[...], dy_ref[...]).astype(BF)


def expert_grads(name, rows, dy, dy_at, q, df):
    return pl.pallas_call(
        expert_grads_kernel,
        name=name,
        out_shape=[
            jax.ShapeDtypeStruct((WIDTH, HIDDEN), BF),
            jax.ShapeDtypeStruct((HIDDEN, WIDTH), BF),
        ],
        grid=(HIDDEN // STEP,),
        in_specs=[
            pl.BlockSpec((FILL, WIDTH), lambda i: (0, 0)),
            pl.BlockSpec((FILL, WIDTH), lambda i: (0, dy_at)),
            pl.BlockSpec((FILL, STEP), lambda i: (0, i)),
            pl.BlockSpec((FILL, STEP), lambda i: (0, i)),
        ],
        out_specs=[
            pl.BlockSpec((WIDTH, STEP), lambda i: (0, i)),
            pl.BlockSpec((STEP, WIDTH), lambda i: (i, 0)),
        ],
        scratch_shapes=[pltpu.VMEM((WIDTH, FILL), BF)],
        compiler_params=pltpu.CompilerParams(vmem_limit_bytes=VMEM),
    )(rows, dy, q, df)


def expert_call(kernel, name, section, core, arrays, weights, outs, kept=()):
    vmem = pl.BlockSpec(memory_space=pltpu.VMEM)
    far = pl.BlockSpec(memory_space=pl.ANY)
    rows_f = pltpu.VMEM((FILL, WIDTH), F32)
    hid = pltpu.VMEM((FILL, HIDDEN), BF)
    first, second = pltpu.VMEM((WIDTH, HIDDEN), BF), pltpu.VMEM((HIDDEN, WIDTH), BF)
    sems = pltpu.SemaphoreType.DMA((2, HIDDEN // STEP))
    scratch = {
        "expert_forward": [first, second, sems, rows_f, hid, hid, sems],
        "expert_both": [first, second, sems, rows_f, rows_f, hid, hid, sems],
        "expert_backward": [first, second, sems, rows_f, hid, sems, hid, sems],
    }[name]
    return pl.pallas_call(
        functools.partial(kernel, section),
        name=name,
        out_shape=[jax.ShapeDtypeStruct(shape, BF) for shape in outs],
        in_specs=[pl.BlockSpec(memory_space=pltpu.SMEM)] + [vmem] * len(arrays) + [far] * (4 + len(kept)),
        out_specs=[vmem] + [far] * (len(outs) - 1),
        scratch_shapes=scratch,
        compiler_params=pltpu.CompilerParams(vmem_limit_bytes=VMEM),
    )(core, *arrays, *weights, *kept)


def pair_sum_kernel(count, core_ref, *refs):
    for i in range(count):
        a, b, c, d = refs[4 * i : 4 * i + 4]
        out = refs[4 * count + i]

        @pl.when(core_ref[0] == 0)
        def _(a=a, b=b, out=out):
            out[...] = (a[...].astype(F32) + b[...].astype(F32)).astype(out.dtype)

        @pl.when(core_ref[0] == 1)
        def _(c=c, d=d, out=out):
            out[...] = (c[...].astype(F32) + d[...].astype(F32)).astype(out.dtype)


def pair_sum(name, core, groups, dtype, steps):
    def spec(shape, section):
        block = (shape[0] // steps,) + shape[1:]

        def index(i, core_ref):
            here = i if section is None else jnp.where(core_ref[0] == section, i, 0)
            return (here,) + (0,) * (len(shape) - 1)

        return pl.BlockSpec(block, index)

    return pl.pallas_call(
        functools.partial(pair_sum_kernel, len(groups)),
        name=name,
        out_shape=[jax.ShapeDtypeStruct(group[0].shape, dtype) for group in groups],
        grid_spec=pltpu.PrefetchScalarGridSpec(
            num_scalar_prefetch=1,
            grid=(steps,),
            in_specs=[spec(group[0].shape, section) for group in groups for section in (0, 0, 1, 1)],
            out_specs=[spec(group[0].shape, None) for group in groups],
        ),
        compiler_params=pltpu.CompilerParams(vmem_limit_bytes=VMEM),
    )(core, *[array for group in groups for array in group])


SWAP = [(0, 1), (1, 0)]
CHIP = ("row", "col")


def swap(values):
    return lax.ppermute(values, "section", SWAP)


def exchange(rows):
    wide = rows.shape[1]
    out = lax.all_to_all(
        rows.reshape(CHIPS, SLOTS, wide), CHIP, split_axis=0, concat_axis=0, tiled=True
    )
    return out.reshape(FILL, wide)


def gather_now(chunk):
    copies = jnp.broadcast_to(chunk[None], (CHIPS,) + chunk.shape)
    return lax.all_to_all(copies, CHIP, split_axis=0, concat_axis=0, tiled=True)


def gather_later(chunk):
    return lax.all_gather(chunk, CHIP, axis=0)


def spread_out(partial):
    return lax.all_to_all(partial, CHIP, split_axis=0, concat_axis=0, tiled=True)


def reduce_step(chunks, mine, stride):
    side = 4
    total = lax.dynamic_index_in_dim(chunks, mine, 0, keepdims=False).astype(F32)
    for turn in range(1, side):
        pairs = []
        for at in range(COLS):
            own = at // stride % side
            pairs.append((at, at + ((own + turn) % side - own) * stride))
        chunk = lax.dynamic_index_in_dim(chunks, (mine + turn) % side, 0, keepdims=False)
        total = total + lax.ppermute(chunk, "col", pairs).astype(F32)
    return total


def reduce_x(values):
    place = lax.axis_index("col")
    chunks = values.reshape((4, 4) + values.shape[1:])
    return reduce_step(chunks, place // 4, 4).astype(BF), place % 4


def add_up(received):
    return jnp.sum(received.astype(F32), axis=0)


def pack(norm_gains, attn_qkv, attn_out, router):
    q, k, v = attn_qkv[0, :, 0], attn_qkv[0, :, 1], attn_qkv[0, :, 2]
    o = attn_out[0].T
    small = jnp.concatenate([router[0], norm_gains[0].T], axis=1)
    small = jnp.pad(small, ((0, 16 - SMALL), (0, 128 - EXPERTS - 2)))
    lo, hi = slice(0, 128), slice(128, 192)
    first = jnp.concatenate([q[:, lo], k[:, lo], v[:, lo], small], axis=0)
    mixed = jnp.concatenate([q[:, hi], k[:, hi]], axis=1)
    last = jnp.concatenate([v[:, hi], o[:, hi]], axis=1)
    second = jnp.concatenate([mixed, o[:, lo], last, small], axis=0)
    return first, second


def unpack(first, second):
    b = [half[i * PART : (i + 1) * PART] for half in (first, second) for i in range(3)]
    q = jnp.concatenate([b[0], b[3][:, :HEAD]], axis=1)
    k = jnp.concatenate([b[1], b[3][:, HEAD:]], axis=1)
    v = jnp.concatenate([b[2], b[5][:, :HEAD]], axis=1)
    o = jnp.concatenate([b[4], b[5][:, HEAD:]], axis=1).T
    small = first[3 * PART : 3 * PART + SMALL]
    gains = small[:, EXPERTS : EXPERTS + 2].T
    return gains[None], jnp.stack([q, k, v], axis=1)[None], o[None], small[None, :, :EXPERTS]


def body(images, cotangent, norm_gains, attn_qkv, attn_out, router, expert_in, expert_out, routes):
    section = lax.axis_index("section")
    core = section.astype(jnp.int32).reshape(1)
    on_first = section == 0

    first, second = pack(norm_gains, attn_qkv, attn_out, router)
    mine = jnp.where(on_first, first, second)
    theirs = swap(jnp.where(on_first, second, first))
    own0 = gather_now(jnp.where(on_first, mine, theirs))
    own1 = gather_later(jnp.where(on_first, theirs, mine))

    w1, w2 = expert_in[0], expert_out[0]
    chosen = jnp.pad(routes[0], ((0, 0), (0, 0), (0, SPAN - SEQ), (0, 126)), constant_values=-1)
    chosen = chosen.reshape(2, PAD, 128)
    own0, w1_other, w2_other, chosen_other = lax.optimization_barrier(
        (own0, swap(w1), swap(w2), swap(chosen))
    )
    routed = (chosen, chosen_other)
    weights = (w1, w1_other, w2, w2_other)
    other0 = swap(own0)

    buf_shape = ((FILL, WIDTH), BF)
    wide_shape = ((FILL, 2 * WIDTH), BF)
    tok_b = ((2, SEQ, WIDTH), BF)
    tok_f = ((2, SEQ, WIDTH), F32)

    buf, *saved0 = whole_call(
        first_kernel, "first", [buf_shape] + SAVED, (core, images, *routed), (own0, other0)
    )
    rows0 = exchange(buf)
    y, q0, gp0 = expert_call(
        expert_forward_kernel, "expert_forward", 0, core, [rows0], weights,
        [(FILL, WIDTH), (FILL, HIDDEN), (FILL, HIDDEN)],
    )
    back = exchange(y)
    own1, _ = lax.optimization_barrier((own1, y))
    other1 = swap(own1)
    h0, c0 = saved0[3], saved0[5]
    x1, y_both, buf, *saved1 = whole_call(
        middle_kernel, "middle", [tok_b, ((PAD, 2 * WIDTH), BF), wide_shape] + SAVED,
        (core, back, h0, c0, *routed, cotangent), (own1, other1),
    )
    rows1 = exchange(buf)
    back, q1, df1 = expert_call(
        expert_both_kernel, "expert_both", 1, core, [rows1], weights,
        [(FILL, 2 * WIDTH), (FILL, HIDDEN), (FILL, HIDDEN)],
    )
    g1_1, g2_1 = expert_grads("expert_grads_1", rows1, rows1, 1, q1, df1)
    to_second, to_first = [(0, 1)], [(1, 0)]
    back, g1_1, g2_1 = lax.optimization_barrier((exchange(back), g1_1, g2_1))
    out_keep, out_send, dx1, ga_keep, ga_send, buf, dgv = whole_call(
        turn_kernel, "turn",
        [tok_b, tok_b, ((PAD, WIDTH), F32), GRADS, GRADS, buf_shape, ((PAD, 128), F32)],
        (core, back, *routed, cotangent, x1, *saved1, y_both, c0), (own1, other1),
    )
    dy0 = exchange(buf)
    partial1 = ga_keep + swap(ga_send)
    partial1, dy0 = lax.optimization_barrier((partial1, dy0))
    rows1_sum = lax.psum_scatter(partial1, "row", scatter_dimension=0, tiled=True)
    back, df0 = expert_call(
        expert_backward_kernel, "expert_backward", 0, core,
        [dy0], weights, [(FILL, WIDTH), (FILL, HIDDEN)], (gp0,),
    )
    g1_0, g2_0 = expert_grads("expert_grads_0", rows0, dy0, 0, q0, df0)
    back, g1_0, g2_0, out_got = lax.optimization_barrier(
        (exchange(back), g1_0, g2_0, swap(out_send))
    )
    r1_1 = lax.ppermute(g1_1, "section", to_second)
    r2_1 = lax.ppermute(g2_1, "section", to_second)
    r1_0 = lax.ppermute(g1_0, "section", to_first)
    r2_0 = lax.ppermute(g2_0, "section", to_first)
    dx_keep, dx_send, ga_keep, ga_send = whole_call(
        last_kernel, "last", [tok_f, tok_f, GRADS, GRADS],
        (core, back, *routed, dx1, dgv, images, *saved0), (own0, other0),
    )
    g1_0, dx_keep, rows1_sum = lax.optimization_barrier((g1_0, dx_keep, rows1_sum))
    planes1_sum, place = reduce_x(rows1_sum)
    partial0, planes1_sum = lax.optimization_barrier((ga_keep + swap(ga_send), planes1_sum))
    received0 = spread_out(partial0)
    total1 = reduce_step(planes1_sum, place, 1)
    grad_first, grad_second = pair_sum(
        "sum_experts", core, [(g1_0, r1_0, g1_1, r1_1), (g2_0, r2_0, g2_1, r2_1)], F32, 6
    )
    received0, grad_first, grad_second, dx_got = lax.optimization_barrier(
        (received0, grad_first, grad_second, swap(dx_send))
    )
    total0 = add_up(received0)

    def order(kept, got):
        return jnp.where(on_first, kept, got), jnp.where(on_first, got, kept)

    section_out = jnp.stack(order(out_keep, out_got))[None]
    input_grads = jnp.stack(order(dx_keep, dx_got))[None]
    kept, sent = jnp.where(on_first, total0, total1), jnp.where(on_first, total1, total0)
    gains, qkv, out, rout = unpack(*order(kept, swap(sent)))
    return (section_out, input_grads, gains, qkv, out, rout, grad_first[None], grad_second[None])


def solution(mesh):
    in_specs = (
        P(None, ("row", "col"), None, None),
        P(None, ("row", "col"), None, None),
        P("section", None, ("row", "col")),
        P("section", "col", None, "row"),
        P("section", "row", "col"),
        P("section", ("row", "col"), None),
        P("section", None, ("row", "col")),
        P("section", ("row", "col"), None),
        P("section", None, ("row", "col"), None, None),
    )
    out_specs = (
        P("section", None, ("row", "col"), None, None),
        P("section", None, ("row", "col"), None, None),
        P("section", None, ("row", "col")),
        P("section", "col", None, "row"),
        P("section", "row", "col"),
        P("section", ("row", "col"), None),
        P("section", None, ("row", "col")),
        P("section", ("row", "col"), None),
    )
    return jax.shard_map(body, mesh=mesh, in_specs=in_specs, out_specs=out_specs, check_vma=False)
```

profile of v0, /device:TPU:1, one launch (start us, length us, event | category | flops | bytes accessed | tf_op | source)
XLA Modules:
  0.0 363.6 jit_solution(5007767249591050620)
XLA Ops:
  7.2 0.8 slice_bitcast_fusion.2
  11.0 1.5 collective-permute-start
  12.5 0.9 collective-permute-done
  13.5 1.8 broadcast_in_dim.30
  15.3 11.3 %all-to-all-start = ((bf16[64,160,128]{2,1,0:T(8,128)(2,1)}), bf16[64,160,128]{2,1,0:T(8,128)(2,1)S(1)}, u32[]{:S(2)}, u32[]{:S(2)}) async-start(bf16[64,160,128]{2,1,0:T(8,128)(2,1)} %broadcast_in_dim.30), calls=%async_computation | async-start | bytes 5242880 | tf_op jit(solution)/shard_map/all_to_all | solution.py:660
  28.9 3.0 collective-permute-done.3.routes_other_ref
  31.9 3.5 collective-permute-done.2.d_ref
  35.5 25.0 %all-to-all-done.own_ref = bf16[64,160,128]{2,1,0:T(8,128)(2,1)S(1)} async-done(((bf16[64,160,128]{2,1,0:T(8,128)(2,1)}), bf16[64,160,128]{2,1,0:T(8,128)(2,1)S(1)}, u32[]{:S(2)}, u32[]{:S(2)}) %all-to-all-start) | async-done | bytes 2621472 | tf_op jit(solution)/shard_map/all_to_all | solution.py:660
  60.5 2.4 collective-permute-start.4
  63.7 3.8 %collective-permute-done.4.other_ref = bf16[64,160,128]{2,1,0:T(8,128)(2,1)S(1)} collective-permute-done((bf16[64,160,128]{2,1,0:T(8,128)(2,1)S(1)}, bf16[64,160,128]{2,1,0:T(8,128)(2,1)S(1)}, u32[]{:S(2)}, u32[]{:S(2)}) %collective-permute-start.4) | collective-permute-done | bytes 2621472 | tf_op jit(solution)/shard_map/ppermute | solution.py:647
  67.4 1.5 copy-done.1
  68.9 8.8 %first.1 = (bf16[512,768]{1,0:T(8,128)(2,1)}, bf16[112,2560]{1,0:T(8,128)(2,1)}, bf16[1344,112]{1,0:T(8,128)(2,1)}, bf16[112,1024]{1,0:T(8,128)(2,1)}, f32[112,7...) custom-call(s32[1]{0:T(128)} %bitcast.core_ref, bf16[2,2,50,768]{3,2,1,0:T(8,128)(2,1)} %copy.19.x_ref, ...), custom_call_target="tpu_custom_call" | custom-call | tf_op jit(solution)/shard_map/first/pallas_call | solution.py:430
  77.8 21.5 %all_to_all.40 = bf16[64,8,768]{2,1,0:T(8,128)(2,1)} all-to-all(bf16[64,8,768]{2,1,0:T(8,128)(2,1)} %bitcast.111), channel_id=1, replica_groups=mesh['section'=2,'row'=4,'col'=16] {'row','col'}, dimensions={0} | all-to-all | bytes 1572864 | tf_op jit(solution)/shard_map/all_to_all | solution.py:652
  99.3 9.6 %expert_forward.1 = (bf16[512,768]{1,0:T(8,128)(2,1)}, bf16[512,1536]{1,0:T(8,128)(2,1)}, bf16[512,1536]{1,0:T(8,128)(2,1)}) custom-call(s32[1]{0:T(128)} %bitcast.core_ref, bf16[512,768]{1,0:T(8,128)(2,1)} %bitcast.94, bf16[768,1536]{1,0:T(8,128)(2,1)} %bitcast.84, bf16[768,1536]{1,0:T(8,128)(2,1)} %collective-permute-done.1.b_ref, ...), custom_call_target="tpu_custom_call" | custom-call | tf_op jit(solution)/shard_map/expert_forward/pallas_call | solution.py:593
  108.9 2.1 collective-permute-start.5
  111.0 5.6 %all-to-all-start.2 = ((bf16[64,8,768]{2,1,0:T(8,128)(2,1)}), bf16[64,8,768]{2,1,0:T(8,128)(2,1)S(1)}, u32[]{:S(2)}, u32[]{:S(2)}) async-start(bf16[64,8,768]{2,1,0:T(8,128)(2,1)} %bitcast.110), calls=%async_computation.2 | async-start | bytes 1572864 | tf_op jit(solution)/shard_map/all_to_all | solution.py:652
  116.6 1.7 copy.20.cot_ref
  118.3 13.6 %all-to-all-done.2 = bf16[64,8,768]{2,1,0:T(8,128)(2,1)S(1)} async-done(((bf16[64,8,768]{2,1,0:T(8,128)(2,1)}), bf16[64,8,768]{2,1,0:T(8,128)(2,1)S(1)}, u32[]{:S(2)}, u32[]{:S(2)}) %all-to-all-start.2) | async-done | bytes 786464 | tf_op jit(solution)/shard_map/all_to_all | solution.py:652
  131.9 0.9 copy-done.6
  132.8 0.8 copy-done.2
  133.6 10.2 %middle.1 = (bf16[2,50,768]{2,1,0:T(8,128)(2,1)}, bf16[112,1536]{1,0:T(8,128)(2,1)}, bf16[512,1536]{1,0:T(8,128)(2,1)}, bf16[112,2560]{1,0:T(8,128)(2,1)}, bf16[...) custom-call(s32[1]{0:T(128)} %bitcast.core_ref, ...), custom_call_target="tpu_custom_call" | custom-call | tf_op jit(solution)/shard_map/middle/pallas_call | solution.py:430
  143.9 27.5 %all_to_all.41 = bf16[64,8,1536]{2,1,0:T(8,128)(2,1)} all-to-all(bf16[64,8,1536]{2,1,0:T(8,128)(2,1)} %bitcast.107), channel_id=1, replica_groups=mesh['section'=2,'row'=4,'col'=16] {'row','col'}, dimensions={0} | all-to-all | bytes 3145728 | tf_op jit(solution)/shard_map/all_to_all | solution.py:652
  171.3 11.3 %expert_both.1 = (bf16[512,1536]{1,0:T(8,128)(2,1)}, bf16[512,1536]{1,0:T(8,128)(2,1)}, bf16[512,1536]{1,0:T(8,128)(2,1)}) custom-call(s32[1]{0:T(128)} %bitcast.core_ref, bf16[512,1536]{1,0:T(8,128)(2,1)} %bitcast.80, bf16[768,1536]{1,0:T(8,128)(2,1)} %bitcast.85, bf16[768,1536]{1,0:T(8,128)(2,1)} %collective-permute-done.1.b_ref, ...), custom_call_target="tpu_custom_call" | custom-call | tf_op jit(solution)/shard_map/expert_both/pallas_call | solution.py:593
  182.6 5.6 %all-to-all-start.4 = ((bf16[64,8,1536]{2,1,0:T(8,128)(2,1)}), bf16[64,8,1536]{2,1,0:T(8,128)(2,1)S(1)}, u32[]{:S(2)}, u32[]{:S(2)}) async-start(bf16[64,8,1536]{2,1,0:T(8,128)(2,1)} %bitcast.106), calls=%async_computation.4 | async-start | bytes 3145728 | tf_op jit(solution)/shard_map/all_to_all | solution.py:652
  188.3 6.3 %expert_grads_1.1 = (bf16[768,1536]{1,0:T(8,128)(2,1)}, bf16[1536,768]{1,0:T(8,128)(2,1)}) custom-call(bf16[512,1536]{1,0:T(8,128)(2,1)} %bitcast.81, bf16[512,1536]{1,0:T(8,128)(2,1)} %bitcast.82, bf16[512,1536]{1,0:T(8,128)(2,1)} %get-tuple-element.83.q_ref, bf16[512,1536]{1,0:T(8,128)(2,1)} %get-tuple-element.84.df_ref), custom_call_target="tpu_custom_call" | custom-call | tf_op jit(solution)/shard_map/expert_grads_1/pallas_call | solution.py:558
  194.6 15.4 %all-to-all-done.4 = bf16[64,8,1536]{2,1,0:T(8,128)(2,1)S(1)} async-done(((bf16[64,8,1536]{2,1,0:T(8,128)(2,1)}), bf16[64,8,1536]{2,1,0:T(8,128)(2,1)S(1)}, u32[]{:S(2)}, u32[]{:S(2)}) %all-to-all-start.4) | async-done | bytes 1572896 | tf_op jit(solution)/shard_map/all_to_all | solution.py:652
  210.0 1.2 copy-done.4
  211.3 13.9 %turn.1 = (bf16[2,50,768]{2,1,0:T(8,128)(2,1)}, bf16[2,50,768]{2,1,0:T(8,128)(2,1)}, f32[112,768]{1,0:T(8,128)}, bf16[64,160,128]{2,1,0:T(8,128)(2,1)}, bf16[64,...) custom-call(s32[1]{0:T(128)} %bitcast.core_ref, bf16[512,1536]{1,0:T(8,128)(2,1)} %bitcast.98, ...), custom_call_target="tpu_custom_call" | custom-call | tf_op jit(solution)/shard_map/turn/pallas_call | solution.py:430
  225.2 3.5 collective-permute-start.6
  228.6 4.6 %all-to-all-start.5 = ((bf16[64,8,768]{2,1,0:T(8,128)(2,1)}), bf16[64,8,768]{2,1,0:T(8,128)(2,1)S(1)}, u32[]{:S(2)}, u32[]{:S(2)}) async-start(bf16[64,8,768]{2,1,0:T(8,128)(2,1)} %bitcast.108), calls=%async_computation.5 | async-start | bytes 1572864 | tf_op jit(solution)/shard_map/all_to_all | solution.py:652
  233.4 3.9 %add.97 = bf16[64,160,128]{2,1,0:T(8,128)(2,1)} add(bf16[64,160,128]{2,1,0:T(8,128)(2,1)} %get-tuple-element.97, bf16[64,160,128]{2,1,0:T(8,128)(2,1)S(1)} %collective-permute-done.6) | non-fusion elementwise | flops 1310720 | bytes 7864320 | tf_op jit(solution)/shard_map/add | solution.py:774
  237.3 11.3 %all-to-all-done.5 = bf16[64,8,768]{2,1,0:T(8,128)(2,1)S(1)} async-done(((bf16[64,8,768]{2,1,0:T(8,128)(2,1)}), bf16[64,8,768]{2,1,0:T(8,128)(2,1)S(1)}, u32[]{:S(2)}, u32[]{:S(2)}) %all-to-all-start.5) | async-done | bytes 786464 | tf_op jit(solution)/shard_map/all_to_all | solution.py:652
  248.6 0.9 copy-done.3
  249.5 8.3 %expert_backward.1 = (bf16[512,768]{1,0:T(8,128)(2,1)}, bf16[512,1536]{1,0:T(8,128)(2,1)}) custom-call(s32[1]{0:T(128)} %bitcast.core_ref, bf16[512,768]{1,0:T(8,128)(2,1)} %bitcast.96, bf16[768,1536]{1,0:T(8,128)(2,1)} %bitcast.86, bf16[768,1536]{1,0:T(8,128)(2,1)} %collective-permute-done.1.b_ref, bf16[1536,768]{1,0:T(8,128)(2,1)} %bitcast.90, ...), custom_call_target="tpu_custom_call" | custom-call | tf_op jit(solution)/shard_map/expert_backward/pallas_call | solution.py:593
  257.8 4.7 %all-to-all-start.6 = ((bf16[64,8,768]{2,1,0:T(8,128)(2,1)}), bf16[64,8,768]{2,1,0:T(8,128)(2,1)S(1)}, u32[]{:S(2)}, u32[]{:S(2)}) async-start(bf16[64,8,768]{2,1,0:T(8,128)(2,1)} %bitcast.109), calls=%async_computation.6 | async-start | bytes 1572864 | tf_op jit(solution)/shard_map/all_to_all | solution.py:652
  262.5 2.5 collective-permute-start.7
  265.0 6.4 %expert_grads_0.1 = (bf16[768,1536]{1,0:T(8,128)(2,1)}, bf16[1536,768]{1,0:T(8,128)(2,1)}) custom-call(bf16[512,768]{1,0:T(8,128)(2,1)} %bitcast.95, bf16[512,768]{1,0:T(8,128)(2,1)} %bitcast.97, bf16[512,1536]{1,0:T(8,128)(2,1)} %get-tuple-element.103.q_ref, bf16[512,1536]{1,0:T(8,128)(2,1)} %get-tuple-element.104.df_ref), custom_call_target="tpu_custom_call" | custom-call | tf_op jit(solution)/shard_map/expert_grads_0/pallas_call | solution.py:558
  271.4 4.8 %all-to-all-done.6 = bf16[64,8,768]{2,1,0:T(8,128)(2,1)S(1)} async-done(((bf16[64,8,768]{2,1,0:T(8,128)(2,1)}), bf16[64,8,768]{2,1,0:T(8,128)(2,1)S(1)}, u32[]{:S(2)}, u32[]{:S(2)}) %all-to-all-start.6) | async-done | bytes 786464 | tf_op jit(solution)/shard_map/all_to_all | solution.py:652
  276.2 0.9 copy-done.5
  277.1 13.3 %last.1 = (f32[2,50,768]{2,1,0:T(8,128)}, f32[2,50,768]{2,1,0:T(8,128)}, bf16[64,160,128]{2,1,0:T(8,128)(2,1)}, bf16[64,160,128]{2,1,0:T(8,128)(2,1)}) custom-call(s32[1]{0:T(128)} %bitcast.core_ref, bf16[512,768]{1,0:T(8,128)(2,1)} %bitcast.99, s32[2,112,128]{2,1,0:T(8,128)} %bitcast.105, s32[2,112,128]{2,1,0:T(8,128)} %copy-done.8, ...), custom_call_target="tpu_custom_call" | custom-call | tf_op jit(solution)/shard_map/last/pallas_call | solution.py:430
  290.4 4.2 %collective-permute-start.8 = (bf16[64,160,128]{2,1,0:T(8,128)(2,1)}, bf16[64,160,128]{2,1,0:T(8,128)(2,1)S(1)}, u32[]{:S(2)}, u32[]{:S(2)}) collective-permute-start(bf16[64,160,128]{2,1,0:T(8,128)(2,1)} %get-tuple-element.121), channel_id=1, source_target_pairs={{0,64},{64,0},{1,65},{65,1},{2,66},{66,2},{3,67},{67,3},{4,68},{68... | collective-permute-start | bytes 7864328 | tf_op jit(solution)/shard_map/ppermute | solution.py:647
  294.7 1.8 dynamic-slice_bitcast_fusion.2
  296.4 1.5 collective-permute-start.10
  297.9 1.1 collective-permute-start.11
  299.4 3.9 %add.98 = bf16[64,160,128]{2,1,0:T(8,128)(2,1)} add(bf16[64,160,128]{2,1,0:T(8,128)(2,1)} %get-tuple-element.120, bf16[64,160,128]{2,1,0:T(8,128)(2,1)S(1)} %collective-permute-done.8) | non-fusion elementwise | flops 1310720 | bytes 7864320 | tf_op jit(solution)/shard_map/add | solution.py:795
  303.8 2.6 collective-permute-done.11
  306.4 1.4 collective-permute-done.9
  307.8 1.1 fusion.2
  308.9 5.9 %all-to-all-start.7 = ((bf16[64,160,128]{2,1,0:T(8,128)(2,1)}), bf16[64,160,128]{2,1,0:T(8,128)(2,1)S(1)}, u32[]{:S(2)}, u32[]{:S(2)}) async-start(bf16[64,160,128]{2,1,0:T(8,128)(2,1)} %add.98), calls=%async_computation.8 | async-start | bytes 5242880 | tf_op jit(solution)/shard_map/all_to_all | solution.py:668
  314.8 1.3 collective-permute-start.13
  316.1 1.3 collective-permute-start.15
  317.4 7.3 %collective-permute-start.12 = (bf16[768,1536]{1,0:T(8,128)(2,1)}, bf16[768,1536]{1,0:T(8,128)(2,1)}, u32[]{:S(2)}, u32[]{:S(2)}) collective-permute-start(bf16[768,1536]{1,0:T(8,128)(2,1)} %get-tuple-element.124.refs_0_), channel_id=1, source_target_pairs={{64,0},{65,1},{66,2},{67,3},{68,4},{69,5},{70,6},{71,7},{72,8},{73... | collective-permute-start | bytes 7077896 | tf_op jit(solution)/shard_map/ppermute | solution.py:787
  324.7 2.7 collective-permute-start.14
  327.5 1.0 copy.24
  328.4 2.7 collective-permute-done.14.refs_5_
  331.2 9.1 %sum_experts.1 = (f32[768,1536]{1,0:T(8,128)}, f32[1536,768]{1,0:T(8,128)}) custom-call(s32[1]{0:T(128)} %bitcast.core_ref, bf16[768,1536]{1,0:T(8,128)(2,1)} %get-tuple-element.124.refs_0_, bf16[768,1536]{1,0:T(8,128)(2,1)} %collective-permute-done.12.refs_1_, bf16[768,1536]{1,0:T(8,128)(2,1)} %get-tuple-element.125.refs_2_, ...), custom_call_target="tpu_custom_call" | custom-call | tf_op jit(solution)/shard_map/sum_experts/pallas_call | solution.py:628
  340.9 1.0 collective-permute-start.17
  341.9 2.4 collective-permute-start.18
  344.3 1.2 collective-permute-start.19
  345.5 2.6 all-to-all-done.7
  348.5 1.0 collective-permute-done.17
  349.9 0.8 broadcast_select_fusion.2
  350.7 1.6 collective-permute-start.20
  352.4 1.1 copy.25
  (79 shorter events, 11.7 us)
Async XLA Ops:
  11.0 2.4 collective-permute-start
  15.3 12.9 %copy-start.12 = (s32[1,2,2,50,2]{3,4,2,1,0:T(2,128)S(1)}, s32[1,2,2,50,2]{3,4,2,1,0:T(2,128)}, u32[]{:S(2)}) copy-start(s32[1,2,2,50,2]{3,4,2,1,0:T(2,128)} %param.17) | copy-start | bytes 4804
  15.3 47.6 %copy-start.10 = (bf16[2,2,50,768]{3,1,2,0:T(2,128)(2,1)S(1)}, bf16[2,2,50,768]{3,1,2,0:T(2,128)(2,1)}, u32[]{:S(2)}) copy-start(bf16[2,2,50,768]{3,1,2,0:T(2,128)(2,1)} %param.9) | copy-start | bytes 921604
  15.3 45.2 %all-to-all-start = ((bf16[64,160,128]{2,1,0:T(8,128)(2,1)}), bf16[64,160,128]{2,1,0:T(8,128)(2,1)S(1)}, u32[]{:S(2)}, u32[]{:S(2)}) async-start(bf16[64,160,128]{2,1,0:T(8,128)(2,1)} %broadcast_in_dim.30), calls=%async_computation | async-start | bytes 5242880 | tf_op jit(solution)/shard_map/all_to_all | solution.py:660
  26.7 82.2 %all-gather.3.cloned.1.call-start = ((), (), s32[]{:S(2)}) async-start(), calls=%async_computation.10 | async-start | bytes 2662400 | tf_op jit(solution)/shard_map/all_gather | solution.py:664
  26.7 5.2 %collective-permute-start.1 = (bf16[768,1536]{1,0:T(8,128)(2,1)}, bf16[768,1536]{1,0:T(8,128)(2,1)}, u32[]{:S(2)}, u32[]{:S(2)}) collective-permute-start(bf16[768,1536]{1,0:T(8,128)(2,1)} %bitcast.83), channel_id=1, source_target_pairs={{0,64},{64,0},{1,65},{65,1},{2,66},{66,2},{3,67},{67,3},{4,68},{68... | collective-permute-start | bytes 7077896 | tf_op jit(solution)/shard_map/ppermute | solution.py:647
  27.4 8.0 %collective-permute-start.2 = (bf16[1536,768]{1,0:T(8,128)(2,1)}, bf16[1536,768]{1,0:T(8,128)(2,1)}, u32[]{:S(2)}, u32[]{:S(2)}) collective-permute-start(bf16[1536,768]{1,0:T(8,128)(2,1)} %bitcast.87), channel_id=1, source_target_pairs={{0,64},{64,0},{1,65},{65,1},{2,66},{66,2},{3,67},{67,3},{4,68},{68... | collective-permute-start | bytes 7077896 | tf_op jit(solution)/shard_map/ppermute | solution.py:647
  28.4 39.0 %copy-start.7 = (s32[2,2,56,128]{3,2,1,0:T(8,128)}, s32[2,2,56,128]{3,2,1,0:T(8,128)S(1)}, u32[]{:S(2)}) copy-start(s32[2,2,56,128]{3,2,1,0:T(8,128)S(1)} %pad.8.clone) | copy-start | bytes 344068
  28.4 3.5 collective-permute-start.3
  31.9 35.5 %copy-start.8 = (s32[2,112,128]{2,1,0:T(8,128)}, s32[2,112,128]{2,1,0:T(8,128)S(1)}, u32[]{:S(2)}) copy-start(s32[2,112,128]{2,1,0:T(8,128)S(1)} %collective-permute-done.3.routes_other_ref) | copy-start | bytes 344068
  60.5 6.9 %copy-start = (bf16[64,160,128]{2,1,0:T(8,128)(2,1)}, bf16[64,160,128]{2,1,0:T(8,128)(2,1)S(1)}, u32[]{:S(2)}) copy-start(bf16[64,160,128]{2,1,0:T(8,128)(2,1)S(1)} %all-to-all-done.own_ref) | copy-start | bytes 7864324
  60.5 6.9 %collective-permute-start.4 = (bf16[64,160,128]{2,1,0:T(8,128)(2,1)S(1)}, bf16[64,160,128]{2,1,0:T(8,128)(2,1)S(1)}, u32[]{:S(2)}, u32[]{:S(2)}) collective-permute-start(bf16[64,160,128]{2,1,0:T(8,128)(2,1)S(1)} %all-to-all-done.own_ref), channel_id=1, source_target_pairs={{0,64},{64,0},{1,65},{65,1},{2,66},{66,2},{3,67},{67,3},{4,68},{68... | collective-permute-start | bytes 7864328 | tf_op jit(solution)/shard_map/ppermute | solution.py:647
  67.4 1.5 copy-start.1
  108.9 23.0 %collective-permute-start.5 = (bf16[64,160,128]{2,1,0:T(8,128)(2,1)}, bf16[64,160,128]{2,1,0:T(8,128)(2,1)S(1)}, u32[]{:S(2)}, u32[]{:S(2)}) collective-permute-start(bf16[64,160,128]{2,1,0:T(8,128)(2,1)} %bitcast.91), channel_id=1, source_target_pairs={{0,64},{64,0},{1,65},{65,1},{2,66},{66,2},{3,67},{67,3},{4,68},{68... | collective-permute-start | bytes 7864328 | tf_op jit(solution)/shard_map/ppermute | solution.py:647
  111.0 20.9 %all-to-all-start.2 = ((bf16[64,8,768]{2,1,0:T(8,128)(2,1)}), bf16[64,8,768]{2,1,0:T(8,128)(2,1)S(1)}, u32[]{:S(2)}, u32[]{:S(2)}) async-start(bf16[64,8,768]{2,1,0:T(8,128)(2,1)} %bitcast.110), calls=%async_computation.2 | async-start | bytes 1572864 | tf_op jit(solution)/shard_map/all_to_all | solution.py:652
  131.9 0.9 copy-start.6
  131.9 1.7 copy-start.2
  182.6 27.4 %all-to-all-start.4 = ((bf16[64,8,1536]{2,1,0:T(8,128)(2,1)}), bf16[64,8,1536]{2,1,0:T(8,128)(2,1)S(1)}, u32[]{:S(2)}, u32[]{:S(2)}) async-start(bf16[64,8,1536]{2,1,0:T(8,128)(2,1)} %bitcast.106), calls=%async_computation.4 | async-start | bytes 3145728 | tf_op jit(solution)/shard_map/all_to_all | solution.py:652
  210.0 1.2 copy-start.4
  225.2 8.2 %collective-permute-start.6 = (bf16[64,160,128]{2,1,0:T(8,128)(2,1)}, bf16[64,160,128]{2,1,0:T(8,128)(2,1)S(1)}, u32[]{:S(2)}, u32[]{:S(2)}) collective-permute-start(bf16[64,160,128]{2,1,0:T(8,128)(2,1)} %get-tuple-element.98), channel_id=1, source_target_pairs={{0,64},{64,0},{1,65},{65,1},{2,66},{66,2},{3,67},{67,3},{4,68},{68... | collective-permute-start | bytes 7864328 | tf_op jit(solution)/shard_map/ppermute | solution.py:647
  228.6 19.9 %all-to-all-start.5 = ((bf16[64,8,768]{2,1,0:T(8,128)(2,1)}), bf16[64,8,768]{2,1,0:T(8,128)(2,1)S(1)}, u32[]{:S(2)}, u32[]{:S(2)}) async-start(bf16[64,8,768]{2,1,0:T(8,128)(2,1)} %bitcast.108), calls=%async_computation.5 | async-start | bytes 1572864 | tf_op jit(solution)/shard_map/all_to_all | solution.py:652
  233.3 61.4 %reduce-scatter.2.cloned.1.call-start = ((), (), s32[]{:S(2)}) async-start(), calls=%async_computation.9 | async-start | bytes 3276800 | tf_op jit(solution)/shard_map/reduce_scatter | solution.py:776
  248.6 0.9 copy-start.3
  249.5 13.0 %copy-start.13 = (bf16[2,50,768]{2,1,0:T(8,128)(2,1)S(1)}, bf16[2,50,768]{2,1,0:T(8,128)(2,1)}, u32[]{:S(2)}) copy-start(bf16[2,50,768]{2,1,0:T(8,128)(2,1)} %get-tuple-element.107) | copy-start | bytes 460804
  257.8 18.4 %all-to-all-start.6 = ((bf16[64,8,768]{2,1,0:T(8,128)(2,1)}), bf16[64,8,768]{2,1,0:T(8,128)(2,1)S(1)}, u32[]{:S(2)}, u32[]{:S(2)}) async-start(bf16[64,8,768]{2,1,0:T(8,128)(2,1)} %bitcast.109), calls=%async_computation.6 | async-start | bytes 1572864 | tf_op jit(solution)/shard_map/all_to_all | solution.py:652
  262.5 8.9 %collective-permute-start.7 = (bf16[2,50,768]{2,1,0:T(8,128)(2,1)S(1)}, bf16[2,50,768]{2,1,0:T(8,128)(2,1)S(1)}, u32[]{:S(2)}, u32[]{:S(2)}) collective-permute-start(bf16[2,50,768]{2,1,0:T(8,128)(2,1)S(1)} %copy-done.13), channel_id=1, source_target_pairs={{0,64},{64,0},{1,65},{65,1},{2,66},{66,2},{3,67},{67,3},{4,68},{68... | collective-permute-start | bytes 460808 | tf_op jit(solution)/shard_map/ppermute | solution.py:647
  276.2 0.9 copy-start.5
  290.4 9.0 %collective-permute-start.8 = (bf16[64,160,128]{2,1,0:T(8,128)(2,1)}, bf16[64,160,128]{2,1,0:T(8,128)(2,1)S(1)}, u32[]{:S(2)}, u32[]{:S(2)}) collective-permute-start(bf16[64,160,128]{2,1,0:T(8,128)(2,1)} %get-tuple-element.121), channel_id=1, source_target_pairs={{0,64},{64,0},{1,65},{65,1},{2,66},{66,2},{3,67},{67,3},{4,68},{68... | collective-permute-start | bytes 7864328 | tf_op jit(solution)/shard_map/ppermute | solution.py:647
  296.4 7.4 %collective-permute-start.10 = (bf16[4,160,128]{2,1,0:T(8,128)(2,1)}, bf16[4,160,128]{2,1,0:T(8,128)(2,1)S(1)}, u32[]{:S(2)}, u32[]{:S(2)}) collective-permute-start(bf16[4,160,128]{2,1,0:T(8,128)(2,1)} %get-tuple-element.150), channel_id=1, source_target_pairs={{0,8},{1,9},{2,10},{3,11},{4,12},{5,13},{6,14},{7,15},{8,0},{9,1},... | collective-permute-start | bytes 491528 | tf_op jit(solution)/shard_map/ppermute | solution.py:680
  297.9 8.5 %collective-permute-start.11 = (bf16[4,160,128]{2,1,0:T(8,128)(2,1)S(1)}, bf16[4,160,128]{2,1,0:T(8,128)(2,1)S(1)}, u32[]{:S(2)}, u32[]{:S(2)}) collective-permute-start(bf16[4,160,128]{2,1,0:T(8,128)(2,1)S(1)} %get-tuple-element.149), channel_id=1, source_target_pairs={{0,12},{1,13},{2,14},{3,15},{4,0},{5,1},{6,2},{7,3},{8,4},{9,5},{1... | collective-permute-start | bytes 491528 | tf_op jit(solution)/shard_map/ppermute | solution.py:680
  299.0 8.8 %collective-permute-start.9 = (bf16[4,160,128]{2,1,0:T(8,128)(2,1)S(1)}, bf16[4,160,128]{2,1,0:T(8,128)(2,1)}, u32[]{:S(2)}, u32[]{:S(2)}) collective-permute-start(bf16[4,160,128]{2,1,0:T(8,128)(2,1)S(1)} %get-tuple-element.148), channel_id=1, source_target_pairs={{0,4},{1,5},{2,6},{3,7},{4,8},{5,9},{6,10},{7,11},{8,12},{9,13},{1... | collective-permute-start | bytes 491528 | tf_op jit(solution)/shard_map/ppermute | solution.py:680
  308.9 18.5 %copy-start.11 = (bf16[2,50,768]{2,1,0:T(8,128)(2,1)S(1)}, bf16[2,50,768]{2,1,0:T(8,128)(2,1)}, u32[]{:S(2)}) copy-start(bf16[2,50,768]{2,1,0:T(8,128)(2,1)} %get-tuple-element.96) | copy-start | bytes 460804
  308.9 39.1 %all-to-all-start.7 = ((bf16[64,160,128]{2,1,0:T(8,128)(2,1)}), bf16[64,160,128]{2,1,0:T(8,128)(2,1)S(1)}, u32[]{:S(2)}, u32[]{:S(2)}) async-start(bf16[64,160,128]{2,1,0:T(8,128)(2,1)} %add.98), calls=%async_computation.8 | async-start | bytes 5242880 | tf_op jit(solution)/shard_map/all_to_all | solution.py:668
  314.8 13.6 %collective-permute-start.13 = (bf16[768,1536]{1,0:T(8,128)(2,1)}, bf16[768,1536]{1,0:T(8,128)(2,1)}, u32[]{:S(2)}, u32[]{:S(2)}) collective-permute-start(bf16[768,1536]{1,0:T(8,128)(2,1)} %get-tuple-element.125.refs_2_), channel_id=1, source_target_pairs={{0,64},{1,65},{2,66},{3,67},{4,68},{5,69},{6,70},{7,71},{8,72},{9,... | collective-permute-start | bytes 7077896 | tf_op jit(solution)/shard_map/ppermute | solution.py:785
  316.1 12.3 %collective-permute-start.15 = (bf16[1536,768]{1,0:T(8,128)(2,1)}, bf16[1536,768]{1,0:T(8,128)(2,1)}, u32[]{:S(2)}, u32[]{:S(2)}) collective-permute-start(bf16[1536,768]{1,0:T(8,128)(2,1)} %get-tuple-element.127.refs_6_), channel_id=1, source_target_pairs={{0,64},{1,65},{2,66},{3,67},{4,68},{5,69},{6,70},{7,71},{8,72},{9,... | collective-permute-start | bytes 7077896 | tf_op jit(solution)/shard_map/ppermute | solution.py:786
  317.4 11.0 %collective-permute-start.12 = (bf16[768,1536]{1,0:T(8,128)(2,1)}, bf16[768,1536]{1,0:T(8,128)(2,1)}, u32[]{:S(2)}, u32[]{:S(2)}) collective-permute-start(bf16[768,1536]{1,0:T(8,128)(2,1)} %get-tuple-element.124.refs_0_), channel_id=1, source_target_pairs={{64,0},{65,1},{66,2},{67,3},{68,4},{69,5},{70,6},{71,7},{72,8},{73... | collective-permute-start | bytes 7077896 | tf_op jit(solution)/shard_map/ppermute | solution.py:787
  324.7 6.4 %collective-permute-start.14 = (bf16[1536,768]{1,0:T(8,128)(2,1)}, bf16[1536,768]{1,0:T(8,128)(2,1)}, u32[]{:S(2)}, u32[]{:S(2)}) collective-permute-start(bf16[1536,768]{1,0:T(8,128)(2,1)} %get-tuple-element.126.refs_4_), channel_id=1, source_target_pairs={{64,0},{65,1},{66,2},{67,3},{68,4},{69,5},{70,6},{71,7},{72,8},{73... | collective-permute-start | bytes 7077896 | tf_op jit(solution)/shard_map/ppermute | solution.py:788
  327.4 18.1 %collective-permute-start.16 = (f32[2,50,768]{2,1,0:T(8,128)}, f32[2,50,768]{2,1,0:T(8,128)S(1)}, u32[]{:S(2)}, u32[]{:S(2)}) collective-permute-start(f32[2,50,768]{2,1,0:T(8,128)} %get-tuple-element.130), channel_id=1, source_target_pairs={{0,64},{64,0},{1,65},{65,1},{2,66},{66,2},{3,67},{67,3},{4,68},{68... | collective-permute-start | bytes 921608 | tf_op jit(solution)/shard_map/ppermute | solution.py:647
  340.3 12.0 %copy-start.9 = (f32[2,50,768]{2,1,0:T(8,128)S(1)}, f32[2,50,768]{2,1,0:T(8,128)}, u32[]{:S(2)}) copy-start(f32[2,50,768]{2,1,0:T(8,128)} %get-tuple-element.119) | copy-start | bytes 921604
  340.9 8.5 %collective-permute-start.17 = (bf16[160,128]{1,0:T(8,128)(2,1)}, bf16[160,128]{1,0:T(8,128)(2,1)S(1)}, u32[]{:S(2)}, u32[]{:S(2)}) collective-permute-start(bf16[160,128]{1,0:T(8,128)(2,1)} %get-tuple-element.155), channel_id=1, source_target_pairs={{0,1},{1,2},{2,3},{3,0},{4,5},{5,6},{6,7},{7,4},{8,9},{9,10},{10,1... | collective-permute-start | bytes 122888 | tf_op jit(solution)/shard_map/ppermute | solution.py:680
  341.9 8.0 %collective-permute-start.18 = (bf16[160,128]{1,0:T(8,128)(2,1)}, bf16[160,128]{1,0:T(8,128)(2,1)S(1)}, u32[]{:S(2)}, u32[]{:S(2)}) collective-permute-start(bf16[160,128]{1,0:T(8,128)(2,1)} %get-tuple-element.157), channel_id=1, source_target_pairs={{0,2},{1,3},{2,0},{3,1},{4,6},{5,7},{6,4},{7,5},{8,10},{9,11},{10,... | collective-permute-start | bytes 122888 | tf_op jit(solution)/shard_map/ppermute | solution.py:680
  344.3 5.6 %collective-permute-start.19 = (bf16[160,128]{1,0:T(8,128)(2,1)}, bf16[160,128]{1,0:T(8,128)(2,1)}, u32[]{:S(2)}, u32[]{:S(2)}) collective-permute-start(bf16[160,128]{1,0:T(8,128)(2,1)} %get-tuple-element.156), channel_id=1, source_target_pairs={{0,3},{1,0},{2,1},{3,2},{4,7},{5,4},{6,5},{7,6},{8,11},{9,8},{10,9... | collective-permute-start | bytes 122888 | tf_op jit(solution)/shard_map/ppermute | solution.py:680
  350.7 2.8 collective-permute-start.20
Sparse Core Ops, SparseCore 0:
  31.0 77.5 all-gather.2
  248.7 39.1 reduce-scatter.1
where the time goes:
time: 371 us; the launch traced here: 364 us
  Pallas kernels  97.4 us (26%)
  waiting for transfers between devices  92.6 us (25%)
  starting transfers between devices  77 us (21%)
  blocking collectives  49 us (13%)
  local copies, waits for them, and re-layouts  19.6 us (5%)
  between operations  14.8 us (4%)
  other arithmetic  13.2 us (4%)
    all_to_all x2, blocking collectives, exchange(): lax.all_to_all(rows.reshape(CHIPS, SLOTS, wide), CHIP, split_axis=0, conc...  49 us
    pallas_call x4, Pallas kernels, whole_call(): pl.pallas_call(kernel, name=name, out_shape=[jax.ShapeDtypeStruct(shape,...  46.3 us
    all_to_all x4, waiting for transfers between devices, exchange(): lax.all_to_all(rows.reshape(CHIPS, SLOTS, wide), CHIP, split_axis=0, conc...  45 us
    pallas_call x3, Pallas kernels, expert_call(): pl.pallas_call(functools.partial(kernel, section), name=name, out_shape=[...  29.2 us
    all_to_all x1, waiting for transfers between devices, gather_now(): return lax.all_to_all(copies, CHIP, split_axis=0, concat_axis=0, tiled=True)  25 us
    all_to_all x4, starting transfers between devices, exchange(): lax.all_to_all(rows.reshape(CHIPS, SLOTS, wide), CHIP, split_axis=0, conc...  20.6 us
    ppermute x11, starting transfers between devices, swap(): return lax.ppermute(values, 'section', SWAP)  19.1 us
    pallas_call x2, Pallas kernels, expert_grads(): pl.pallas_call(expert_grads_kernel, name=name, out_shape=[jax.ShapeDtypeS...  12.7 us
  transfers between devices with their start and end apart: 29, of which 16 were waited for; matrix products, arithmetic and copies ran while one was open for 4% of the time, Pallas kernels for 17%

commit v1 on v0

--- a/solution.py
+++ b/solution.py
@@ -303,13 +303,12 @@
     return dx, (a, db, dl, terms1, (dn * unit).astype(BF))
 
 
-def ship(core, g_ref, keep_ref, send_ref, sems):
-    copies = send([
-        (g_ref.at[1 - core], send_ref, sems.at[0]),
-        (g_ref.at[core], keep_ref, sems.at[1]),
+def ship(core, rows, part, g_ref, keep_ref, send_ref, sems):
+    here = (slice(0, CHIPS), rows)
+    return send([
+        (g_ref.at[(1 - core,) + here], send_ref.at[here], sems.at[0, part]),
+        (g_ref.at[(core,) + here], keep_ref.at[here], sems.at[1, part]),
     ])
-    for copy in copies:
-        copy.wait()
 
 
 def gate_grads(dz, y_both, marks):
@@ -384,17 +383,23 @@
     dz = read_tokens(cot_ref.at[core])
     dgv = gate_grads(dz, y_both, marks)
 
+    copies = []
+
     def take(r, a, db, dm):
         projection_grads(r, a, db, dm, o_ref[:, r * 256 : (r + 1) * 256], g_ref)
+        if r == ROWS - 1:
+            copies.extend(ship(core, slice(0, 3 * PART), 0, g_ref, gk_ref, gs_ref, sems))
 
     dx, terms = layer_backward(dz, back_ref[:, WIDTH:], marks, dgv, x, h, chance, small, gain1, gain2, wait, read, m_ref, p_ref, o_ref, take)
     dx_ref[...] = dx
     small_grads(b_ref[...], *terms[2:], g_ref)
+    copies += ship(core, slice(3 * PART, 3 * PART + 16), 1, g_ref, gk_ref, gs_ref, sems)
     dz = dx.astype(BF).astype(F32)
     marks = routing(core, 0, routes_ref, routes_other_ref)
     buf_ref[...] = grad_rows(dz, c0_ref[...], marks)
     dgv_ref[...] = gate_grads(dz, y0_ref[...], marks)
-    ship(core, g_ref, gk_ref, gs_ref, sems)
+    for copy in copies:
+        copy.wait()
 
 
 def last_kernel(core_ref, back_ref, routes_ref, routes_other_ref, dz_ref, dgv_ref, x_ref, m_ref, p_ref, o_ref, h_ref, b_ref, c_ref, own_ref, other_ref, keep_ref, send_ref, gk_ref, gs_ref, w_ref, small_ref, w_sems, g_ref, sems):
@@ -406,15 +411,21 @@
     dx1 = dz_ref[...]
     dz = dx1.astype(BF).astype(F32)
 
+    copies = []
+
     def take(r, a, db, dm):
         projection_grads(r, a, db, dm, o_ref[:, r * 256 : (r + 1) * 256], g_ref)
+        if r == ROWS - 1:
+            copies.extend(ship(core, slice(0, 3 * PART), 0, g_ref, gk_ref, gs_ref, sems))
 
     dx, terms = layer_backward(dz, back_ref[...], marks, dgv_ref[...], read_tokens(x_ref.at[core]), h_ref[...], c_ref[...], small, gain1, gain2, wait, read, m_ref, p_ref, o_ref, take)
     small_grads(b_ref[...], *terms[2:], g_ref)
+    copies += ship(core, slice(3 * PART, 3 * PART + 16), 1, g_ref, gk_ref, gs_ref, sems)
     on_first = core == 0
     write_tokens(keep_ref, jnp.where(on_first, dx, dx1))
     write_tokens(send_ref, jnp.where(on_first, dx1, dx))
-    ship(core, g_ref, gk_ref, gs_ref, sems)
+    for copy in copies:
+        copy.wait()
 
 
 def whole_call(kernel, name, outs, args, weights):
@@ -426,7 +437,7 @@
         pltpu.SemaphoreType.DMA((7, ROWS)),
     ]
     if GRADS in outs:
-        scratch += [pltpu.VMEM((2,) + GRADS[0], BF), pltpu.SemaphoreType.DMA((2,))]
+        scratch += [pltpu.VMEM((2,) + GRADS[0], BF), pltpu.SemaphoreType.DMA((2, 2))]
     return pl.pallas_call(
         kernel,
         name=name,

time: 371 us -> 370 us (level)
  no operation moved by 1% of the time
where the time goes in v1:
time: 370 us; the launch traced here: 363 us
  Pallas kernels  96.6 us (26%)
  waiting for transfers between devices  92.6 us (25%)
  starting transfers between devices  77.1 us (21%)
  blocking collectives  49 us (13%)
  local copies, waits for them, and re-layouts  19.6 us (5%)
  between operations  14.8 us (4%)
  other arithmetic  13.2 us (4%)
    all_to_all x2, blocking collectives, exchange(): lax.all_to_all(rows.reshape(CHIPS, SLOTS, wide), CHIP, split_axis=0, conc...  49 us
    pallas_call x4, Pallas kernels, whole_call(): pl.pallas_call(kernel, name=name, out_shape=[jax.ShapeDtypeStruct(shape,...  45.5 us
    all_to_all x4, waiting for transfers between devices, exchange(): lax.all_to_all(rows.reshape(CHIPS, SLOTS, wide), CHIP, split_axis=0, conc...  45 us
    pallas_call x3, Pallas kernels, expert_call(): pl.pallas_call(functools.partial(kernel, section), name=name, out_shape=[...  29.2 us
    all_to_all x1, waiting for transfers between devices, gather_now(): return lax.all_to_all(copies, CHIP, split_axis=0, concat_axis=0, tiled=True)  25 us
    all_to_all x4, starting transfers between devices, exchange(): lax.all_to_all(rows.reshape(CHIPS, SLOTS, wide), CHIP, split_axis=0, conc...  20.6 us
    ppermute x11, starting transfers between devices, swap(): return lax.ppermute(values, 'section', SWAP)  19.1 us
    pallas_call x2, Pallas kernels, expert_grads(): pl.pallas_call(expert_grads_kernel, name=name, out_shape=[jax.ShapeDtypeS...  12.7 us
  transfers between devices with their start and end apart: 29, of which 16 were waited for; matrix products, arithmetic and copies ran while one was open for 4% of the time, Pallas kernels for 17%

profile of v1, /device:TPU:1, one launch (start us, length us, event | category | flops | bytes accessed | tf_op | source)
XLA Modules:
  0.0 362.8 jit_solution(7114300333637035914)
XLA Ops:
  7.2 0.8 slice_bitcast_fusion.2
  11.0 1.5 collective-permute-start
  12.5 0.9 collective-permute-done
  13.5 1.8 broadcast_in_dim.30
  15.3 11.3 %all-to-all-start = ((bf16[64,160,128]{2,1,0:T(8,128)(2,1)}), bf16[64,160,128]{2,1,0:T(8,128)(2,1)S(1)}, u32[]{:S(2)}, u32[]{:S(2)}) async-start(bf16[64,160,128]{2,1,0:T(8,128)(2,1)} %broadcast_in_dim.30), calls=%async_computation | async-start | bytes 5242880 | tf_op jit(solution)/shard_map/all_to_all | solution.py:671
  28.9 3.0 collective-permute-done.3.routes_other_ref
  31.9 3.5 collective-permute-done.2.d_ref
  35.5 25.0 %all-to-all-done.own_ref = bf16[64,160,128]{2,1,0:T(8,128)(2,1)S(1)} async-done(((bf16[64,160,128]{2,1,0:T(8,128)(2,1)}), bf16[64,160,128]{2,1,0:T(8,128)(2,1)S(1)}, u32[]{:S(2)}, u32[]{:S(2)}) %all-to-all-start) | async-done | bytes 2621472 | tf_op jit(solution)/shard_map/all_to_all | solution.py:671
  60.5 2.4 collective-permute-start.4
  63.7 3.8 %collective-permute-done.4.other_ref = bf16[64,160,128]{2,1,0:T(8,128)(2,1)S(1)} collective-permute-done((bf16[64,160,128]{2,1,0:T(8,128)(2,1)S(1)}, bf16[64,160,128]{2,1,0:T(8,128)(2,1)S(1)}, u32[]{:S(2)}, u32[]{:S(2)}) %collective-permute-start.4) | collective-permute-done | bytes 2621472 | tf_op jit(solution)/shard_map/ppermute | solution.py:658
  67.4 1.5 copy-done.1
  68.9 8.8 %first.1 = (bf16[512,768]{1,0:T(8,128)(2,1)}, bf16[112,2560]{1,0:T(8,128)(2,1)}, bf16[1344,112]{1,0:T(8,128)(2,1)}, bf16[112,1024]{1,0:T(8,128)(2,1)}, f32[112,7...) custom-call(s32[1]{0:T(128)} %bitcast.core_ref, bf16[2,2,50,768]{3,2,1,0:T(8,128)(2,1)} %copy.19.x_ref, ...), custom_call_target="tpu_custom_call" | custom-call | tf_op jit(solution)/shard_map/first/pallas_call | solution.py:441
  77.8 21.5 %all_to_all.40 = bf16[64,8,768]{2,1,0:T(8,128)(2,1)} all-to-all(bf16[64,8,768]{2,1,0:T(8,128)(2,1)} %bitcast.111), channel_id=1, replica_groups=mesh['section'=2,'row'=4,'col'=16] {'row','col'}, dimensions={0} | all-to-all | bytes 1572864 | tf_op jit(solution)/shard_map/all_to_all | solution.py:663
  99.3 9.6 %expert_forward.1 = (bf16[512,768]{1,0:T(8,128)(2,1)}, bf16[512,1536]{1,0:T(8,128)(2,1)}, bf16[512,1536]{1,0:T(8,128)(2,1)}) custom-call(s32[1]{0:T(128)} %bitcast.core_ref, bf16[512,768]{1,0:T(8,128)(2,1)} %bitcast.94, bf16[768,1536]{1,0:T(8,128)(2,1)} %bitcast.84, bf16[768,1536]{1,0:T(8,128)(2,1)} %collective-permute-done.1.b_ref, ...), custom_call_target="tpu_custom_call" | custom-call | tf_op jit(solution)/shard_map/expert_forward/pallas_call | solution.py:604
  108.9 2.1 collective-permute-start.5
  111.0 5.6 %all-to-all-start.2 = ((bf16[64,8,768]{2,1,0:T(8,128)(2,1)}), bf16[64,8,768]{2,1,0:T(8,128)(2,1)S(1)}, u32[]{:S(2)}, u32[]{:S(2)}) async-start(bf16[64,8,768]{2,1,0:T(8,128)(2,1)} %bitcast.110), calls=%async_computation.2 | async-start | bytes 1572864 | tf_op jit(solution)/shard_map/all_to_all | solution.py:663
  116.6 1.7 copy.20.cot_ref
  118.3 13.6 %all-to-all-done.2 = bf16[64,8,768]{2,1,0:T(8,128)(2,1)S(1)} async-done(((bf16[64,8,768]{2,1,0:T(8,128)(2,1)}), bf16[64,8,768]{2,1,0:T(8,128)(2,1)S(1)}, u32[]{:S(2)}, u32[]{:S(2)}) %all-to-all-start.2) | async-done | bytes 786464 | tf_op jit(solution)/shard_map/all_to_all | solution.py:663
  131.9 0.9 copy-done.6
  132.8 0.8 copy-done.2
  133.6 10.2 %middle.1 = (bf16[2,50,768]{2,1,0:T(8,128)(2,1)}, bf16[112,1536]{1,0:T(8,128)(2,1)}, bf16[512,1536]{1,0:T(8,128)(2,1)}, bf16[112,2560]{1,0:T(8,128)(2,1)}, bf16[...) custom-call(s32[1]{0:T(128)} %bitcast.core_ref, ...), custom_call_target="tpu_custom_call" | custom-call | tf_op jit(solution)/shard_map/middle/pallas_call | solution.py:441
  143.9 27.5 %all_to_all.41 = bf16[64,8,1536]{2,1,0:T(8,128)(2,1)} all-to-all(bf16[64,8,1536]{2,1,0:T(8,128)(2,1)} %bitcast.107), channel_id=1, replica_groups=mesh['section'=2,'row'=4,'col'=16] {'row','col'}, dimensions={0} | all-to-all | bytes 3145728 | tf_op jit(solution)/shard_map/all_to_all | solution.py:663
  171.3 11.3 %expert_both.1 = (bf16[512,1536]{1,0:T(8,128)(2,1)}, bf16[512,1536]{1,0:T(8,128)(2,1)}, bf16[512,1536]{1,0:T(8,128)(2,1)}) custom-call(s32[1]{0:T(128)} %bitcast.core_ref, bf16[512,1536]{1,0:T(8,128)(2,1)} %bitcast.80, bf16[768,1536]{1,0:T(8,128)(2,1)} %bitcast.85, bf16[768,1536]{1,0:T(8,128)(2,1)} %collective-permute-done.1.b_ref, ...), custom_call_target="tpu_custom_call" | custom-call | tf_op jit(solution)/shard_map/expert_both/pallas_call | solution.py:604
  182.6 5.6 %all-to-all-start.4 = ((bf16[64,8,1536]{2,1,0:T(8,128)(2,1)}), bf16[64,8,1536]{2,1,0:T(8,128)(2,1)S(1)}, u32[]{:S(2)}, u32[]{:S(2)}) async-start(bf16[64,8,1536]{2,1,0:T(8,128)(2,1)} %bitcast.106), calls=%async_computation.4 | async-start | bytes 3145728 | tf_op jit(solution)/shard_map/all_to_all | solution.py:663
  188.3 6.3 %expert_grads_1.1 = (bf16[768,1536]{1,0:T(8,128)(2,1)}, bf16[1536,768]{1,0:T(8,128)(2,1)}) custom-call(bf16[512,1536]{1,0:T(8,128)(2,1)} %bitcast.81, bf16[512,1536]{1,0:T(8,128)(2,1)} %bitcast.82, bf16[512,1536]{1,0:T(8,128)(2,1)} %get-tuple-element.83.q_ref, bf16[512,1536]{1,0:T(8,128)(2,1)} %get-tuple-element.84.df_ref), custom_call_target="tpu_custom_call" | custom-call | tf_op jit(solution)/shard_map/expert_grads_1/pallas_call | solution.py:569
  194.6 15.4 %all-to-all-done.4 = bf16[64,8,1536]{2,1,0:T(8,128)(2,1)S(1)} async-done(((bf16[64,8,1536]{2,1,0:T(8,128)(2,1)}), bf16[64,8,1536]{2,1,0:T(8,128)(2,1)S(1)}, u32[]{:S(2)}, u32[]{:S(2)}) %all-to-all-start.4) | async-done | bytes 1572896 | tf_op jit(solution)/shard_map/all_to_all | solution.py:663
  210.0 1.2 copy-done.4
  211.3 13.5 %turn.1 = (bf16[2,50,768]{2,1,0:T(8,128)(2,1)}, bf16[2,50,768]{2,1,0:T(8,128)(2,1)}, f32[112,768]{1,0:T(8,128)}, bf16[64,160,128]{2,1,0:T(8,128)(2,1)}, bf16[64,...) custom-call(s32[1]{0:T(128)} %bitcast.core_ref, bf16[512,1536]{1,0:T(8,128)(2,1)} %bitcast.98, ...), custom_call_target="tpu_custom_call" | custom-call | tf_op jit(solution)/shard_map/turn/pallas_call | solution.py:441
  224.8 3.5 collective-permute-start.6
  228.2 4.6 %all-to-all-start.5 = ((bf16[64,8,768]{2,1,0:T(8,128)(2,1)}), bf16[64,8,768]{2,1,0:T(8,128)(2,1)S(1)}, u32[]{:S(2)}, u32[]{:S(2)}) async-start(bf16[64,8,768]{2,1,0:T(8,128)(2,1)} %bitcast.108), calls=%async_computation.5 | async-start | bytes 1572864 | tf_op jit(solution)/shard_map/all_to_all | solution.py:663
  233.0 3.9 %add.97 = bf16[64,160,128]{2,1,0:T(8,128)(2,1)} add(bf16[64,160,128]{2,1,0:T(8,128)(2,1)} %get-tuple-element.97, bf16[64,160,128]{2,1,0:T(8,128)(2,1)S(1)} %collective-permute-done.6) | non-fusion elementwise | flops 1310720 | bytes 7864320 | tf_op jit(solution)/shard_map/add | solution.py:785
  236.8 11.3 %all-to-all-done.5 = bf16[64,8,768]{2,1,0:T(8,128)(2,1)S(1)} async-done(((bf16[64,8,768]{2,1,0:T(8,128)(2,1)}), bf16[64,8,768]{2,1,0:T(8,128)(2,1)S(1)}, u32[]{:S(2)}, u32[]{:S(2)}) %all-to-all-start.5) | async-done | bytes 786464 | tf_op jit(solution)/shard_map/all_to_all | solution.py:663
  248.2 0.9 copy-done.3
  249.1 8.3 %expert_backward.1 = (bf16[512,768]{1,0:T(8,128)(2,1)}, bf16[512,1536]{1,0:T(8,128)(2,1)}) custom-call(s32[1]{0:T(128)} %bitcast.core_ref, bf16[512,768]{1,0:T(8,128)(2,1)} %bitcast.96, bf16[768,1536]{1,0:T(8,128)(2,1)} %bitcast.86, bf16[768,1536]{1,0:T(8,128)(2,1)} %collective-permute-done.1.b_ref, bf16[1536,768]{1,0:T(8,128)(2,1)} %bitcast.90, ...), custom_call_target="tpu_custom_call" | custom-call | tf_op jit(solution)/shard_map/expert_backward/pallas_call | solution.py:604
  257.4 4.7 %all-to-all-start.6 = ((bf16[64,8,768]{2,1,0:T(8,128)(2,1)}), bf16[64,8,768]{2,1,0:T(8,128)(2,1)S(1)}, u32[]{:S(2)}, u32[]{:S(2)}) async-start(bf16[64,8,768]{2,1,0:T(8,128)(2,1)} %bitcast.109), calls=%async_computation.6 | async-start | bytes 1572864 | tf_op jit(solution)/shard_map/all_to_all | solution.py:663
  262.1 2.6 collective-permute-start.7
  264.6 6.4 %expert_grads_0.1 = (bf16[768,1536]{1,0:T(8,128)(2,1)}, bf16[1536,768]{1,0:T(8,128)(2,1)}) custom-call(bf16[512,768]{1,0:T(8,128)(2,1)} %bitcast.95, bf16[512,768]{1,0:T(8,128)(2,1)} %bitcast.97, bf16[512,1536]{1,0:T(8,128)(2,1)} %get-tuple-element.103.q_ref, bf16[512,1536]{1,0:T(8,128)(2,1)} %get-tuple-element.104.df_ref), custom_call_target="tpu_custom_call" | custom-call | tf_op jit(solution)/shard_map/expert_grads_0/pallas_call | solution.py:569
  271.0 4.8 %all-to-all-done.6 = bf16[64,8,768]{2,1,0:T(8,128)(2,1)S(1)} async-done(((bf16[64,8,768]{2,1,0:T(8,128)(2,1)}), bf16[64,8,768]{2,1,0:T(8,128)(2,1)S(1)}, u32[]{:S(2)}, u32[]{:S(2)}) %all-to-all-start.6) | async-done | bytes 786464 | tf_op jit(solution)/shard_map/all_to_all | solution.py:663
  275.8 0.9 copy-done.5
  276.7 12.9 %last.1 = (f32[2,50,768]{2,1,0:T(8,128)}, f32[2,50,768]{2,1,0:T(8,128)}, bf16[64,160,128]{2,1,0:T(8,128)(2,1)}, bf16[64,160,128]{2,1,0:T(8,128)(2,1)}) custom-call(s32[1]{0:T(128)} %bitcast.core_ref, bf16[512,768]{1,0:T(8,128)(2,1)} %bitcast.99, s32[2,112,128]{2,1,0:T(8,128)} %bitcast.105, s32[2,112,128]{2,1,0:T(8,128)} %copy-done.8, ...), custom_call_target="tpu_custom_call" | custom-call | tf_op jit(solution)/shard_map/last/pallas_call | solution.py:441
  289.6 4.2 %collective-permute-start.8 = (bf16[64,160,128]{2,1,0:T(8,128)(2,1)}, bf16[64,160,128]{2,1,0:T(8,128)(2,1)S(1)}, u32[]{:S(2)}, u32[]{:S(2)}) collective-permute-start(bf16[64,160,128]{2,1,0:T(8,128)(2,1)} %get-tuple-element.121), channel_id=1, source_target_pairs={{0,64},{64,0},{1,65},{65,1},{2,66},{66,2},{3,67},{67,3},{4,68},{68... | collective-permute-start | bytes 7864328 | tf_op jit(solution)/shard_map/ppermute | solution.py:658
  293.8 1.8 dynamic-slice_bitcast_fusion.2
  295.6 1.5 collective-permute-start.10
  297.1 1.1 collective-permute-start.11
  298.6 3.9 %add.98 = bf16[64,160,128]{2,1,0:T(8,128)(2,1)} add(bf16[64,160,128]{2,1,0:T(8,128)(2,1)} %get-tuple-element.120, bf16[64,160,128]{2,1,0:T(8,128)(2,1)S(1)} %collective-permute-done.8) | non-fusion elementwise | flops 1310720 | bytes 7864320 | tf_op jit(solution)/shard_map/add | solution.py:806
  303.0 2.6 collective-permute-done.11
  305.6 1.4 collective-permute-done.9
  307.0 1.1 fusion.2
  308.1 5.9 %all-to-all-start.7 = ((bf16[64,160,128]{2,1,0:T(8,128)(2,1)}), bf16[64,160,128]{2,1,0:T(8,128)(2,1)S(1)}, u32[]{:S(2)}, u32[]{:S(2)}) async-start(bf16[64,160,128]{2,1,0:T(8,128)(2,1)} %add.98), calls=%async_computation.8 | async-start | bytes 5242880 | tf_op jit(solution)/shard_map/all_to_all | solution.py:679
  314.0 1.3 collective-permute-start.13
  315.3 1.3 collective-permute-start.15
  316.6 7.3 %collective-permute-start.12 = (bf16[768,1536]{1,0:T(8,128)(2,1)}, bf16[768,1536]{1,0:T(8,128)(2,1)}, u32[]{:S(2)}, u32[]{:S(2)}) collective-permute-start(bf16[768,1536]{1,0:T(8,128)(2,1)} %get-tuple-element.124.refs_0_), channel_id=1, source_target_pairs={{64,0},{65,1},{66,2},{67,3},{68,4},{69,5},{70,6},{71,7},{72,8},{73... | collective-permute-start | bytes 7077896 | tf_op jit(solution)/shard_map/ppermute | solution.py:798
  323.9 2.7 collective-permute-start.14
  326.7 1.0 copy.24
  327.6 2.7 collective-permute-done.14.refs_5_
  330.3 9.1 %sum_experts.1 = (f32[768,1536]{1,0:T(8,128)}, f32[1536,768]{1,0:T(8,128)}) custom-call(s32[1]{0:T(128)} %bitcast.core_ref, bf16[768,1536]{1,0:T(8,128)(2,1)} %get-tuple-element.124.refs_0_, bf16[768,1536]{1,0:T(8,128)(2,1)} %collective-permute-done.12.refs_1_, bf16[768,1536]{1,0:T(8,128)(2,1)} %get-tuple-element.125.refs_2_, ...), custom_call_target="tpu_custom_call" | custom-call | tf_op jit(solution)/shard_map/sum_experts/pallas_call | solution.py:639
  340.1 1.0 collective-permute-start.17
  341.1 2.4 collective-permute-start.18
  343.5 1.2 collective-permute-start.19
  344.7 2.6 all-to-all-done.7
  347.6 1.0 collective-permute-done.17
  349.1 0.8 broadcast_select_fusion.2
  349.9 1.6 collective-permute-start.20
  351.6 1.1 copy.25
  (79 shorter events, 11.6 us)
Async XLA Ops:
  11.0 2.4 collective-permute-start
  15.3 12.9 %copy-start.12 = (s32[1,2,2,50,2]{3,4,2,1,0:T(2,128)S(1)}, s32[1,2,2,50,2]{3,4,2,1,0:T(2,128)}, u32[]{:S(2)}) copy-start(s32[1,2,2,50,2]{3,4,2,1,0:T(2,128)} %param.17) | copy-start | bytes 4804
  15.3 47.6 %copy-start.10 = (bf16[2,2,50,768]{3,1,2,0:T(2,128)(2,1)S(1)}, bf16[2,2,50,768]{3,1,2,0:T(2,128)(2,1)}, u32[]{:S(2)}) copy-start(bf16[2,2,50,768]{3,1,2,0:T(2,128)(2,1)} %param.9) | copy-start | bytes 921604
  15.3 45.2 %all-to-all-start = ((bf16[64,160,128]{2,1,0:T(8,128)(2,1)}), bf16[64,160,128]{2,1,0:T(8,128)(2,1)S(1)}, u32[]{:S(2)}, u32[]{:S(2)}) async-start(bf16[64,160,128]{2,1,0:T(8,128)(2,1)} %broadcast_in_dim.30), calls=%async_computation | async-start | bytes 5242880 | tf_op jit(solution)/shard_map/all_to_all | solution.py:671
  26.7 82.2 %all-gather.3.cloned.1.call-start = ((), (), s32[]{:S(2)}) async-start(), calls=%async_computation.10 | async-start | bytes 2662400 | tf_op jit(solution)/shard_map/all_gather | solution.py:675
  26.7 5.2 %collective-permute-start.1 = (bf16[768,1536]{1,0:T(8,128)(2,1)}, bf16[768,1536]{1,0:T(8,128)(2,1)}, u32[]{:S(2)}, u32[]{:S(2)}) collective-permute-start(bf16[768,1536]{1,0:T(8,128)(2,1)} %bitcast.83), channel_id=1, source_target_pairs={{0,64},{64,0},{1,65},{65,1},{2,66},{66,2},{3,67},{67,3},{4,68},{68... | collective-permute-start | bytes 7077896 | tf_op jit(solution)/shard_map/ppermute | solution.py:658
  27.4 8.0 %collective-permute-start.2 = (bf16[1536,768]{1,0:T(8,128)(2,1)}, bf16[1536,768]{1,0:T(8,128)(2,1)}, u32[]{:S(2)}, u32[]{:S(2)}) collective-permute-start(bf16[1536,768]{1,0:T(8,128)(2,1)} %bitcast.87), channel_id=1, source_target_pairs={{0,64},{64,0},{1,65},{65,1},{2,66},{66,2},{3,67},{67,3},{4,68},{68... | collective-permute-start | bytes 7077896 | tf_op jit(solution)/shard_map/ppermute | solution.py:658
  28.4 39.0 %copy-start.7 = (s32[2,2,56,128]{3,2,1,0:T(8,128)}, s32[2,2,56,128]{3,2,1,0:T(8,128)S(1)}, u32[]{:S(2)}) copy-start(s32[2,2,56,128]{3,2,1,0:T(8,128)S(1)} %pad.8.clone) | copy-start | bytes 344068
  28.4 3.5 collective-permute-start.3
  31.9 35.5 %copy-start.8 = (s32[2,112,128]{2,1,0:T(8,128)}, s32[2,112,128]{2,1,0:T(8,128)S(1)}, u32[]{:S(2)}) copy-start(s32[2,112,128]{2,1,0:T(8,128)S(1)} %collective-permute-done.3.routes_other_ref) | copy-start | bytes 344068
  60.5 6.9 %copy-start = (bf16[64,160,128]{2,1,0:T(8,128)(2,1)}, bf16[64,160,128]{2,1,0:T(8,128)(2,1)S(1)}, u32[]{:S(2)}) copy-start(bf16[64,160,128]{2,1,0:T(8,128)(2,1)S(1)} %all-to-all-done.own_ref) | copy-start | bytes 7864324
  60.5 6.9 %collective-permute-start.4 = (bf16[64,160,128]{2,1,0:T(8,128)(2,1)S(1)}, bf16[64,160,128]{2,1,0:T(8,128)(2,1)S(1)}, u32[]{:S(2)}, u32[]{:S(2)}) collective-permute-start(bf16[64,160,128]{2,1,0:T(8,128)(2,1)S(1)} %all-to-all-done.own_ref), channel_id=1, source_target_pairs={{0,64},{64,0},{1,65},{65,1},{2,66},{66,2},{3,67},{67,3},{4,68},{68... | collective-permute-start | bytes 7864328 | tf_op jit(solution)/shard_map/ppermute | solution.py:658
  67.4 1.5 copy-start.1
  108.9 23.0 %collective-permute-start.5 = (bf16[64,160,128]{2,1,0:T(8,128)(2,1)}, bf16[64,160,128]{2,1,0:T(8,128)(2,1)S(1)}, u32[]{:S(2)}, u32[]{:S(2)}) collective-permute-start(bf16[64,160,128]{2,1,0:T(8,128)(2,1)} %bitcast.91), channel_id=1, source_target_pairs={{0,64},{64,0},{1,65},{65,1},{2,66},{66,2},{3,67},{67,3},{4,68},{68... | collective-permute-start | bytes 7864328 | tf_op jit(solution)/shard_map/ppermute | solution.py:658
  111.0 20.9 %all-to-all-start.2 = ((bf16[64,8,768]{2,1,0:T(8,128)(2,1)}), bf16[64,8,768]{2,1,0:T(8,128)(2,1)S(1)}, u32[]{:S(2)}, u32[]{:S(2)}) async-start(bf16[64,8,768]{2,1,0:T(8,128)(2,1)} %bitcast.110), calls=%async_computation.2 | async-start | bytes 1572864 | tf_op jit(solution)/shard_map/all_to_all | solution.py:663
  131.9 0.9 copy-start.6
  131.9 1.7 copy-start.2
  182.6 27.4 %all-to-all-start.4 = ((bf16[64,8,1536]{2,1,0:T(8,128)(2,1)}), bf16[64,8,1536]{2,1,0:T(8,128)(2,1)S(1)}, u32[]{:S(2)}, u32[]{:S(2)}) async-start(bf16[64,8,1536]{2,1,0:T(8,128)(2,1)} %bitcast.106), calls=%async_computation.4 | async-start | bytes 3145728 | tf_op jit(solution)/shard_map/all_to_all | solution.py:663
  210.0 1.2 copy-start.4
  224.8 8.2 %collective-permute-start.6 = (bf16[64,160,128]{2,1,0:T(8,128)(2,1)}, bf16[64,160,128]{2,1,0:T(8,128)(2,1)S(1)}, u32[]{:S(2)}, u32[]{:S(2)}) collective-permute-start(bf16[64,160,128]{2,1,0:T(8,128)(2,1)} %get-tuple-element.98), channel_id=1, source_target_pairs={{0,64},{64,0},{1,65},{65,1},{2,66},{66,2},{3,67},{67,3},{4,68},{68... | collective-permute-start | bytes 7864328 | tf_op jit(solution)/shard_map/ppermute | solution.py:658
  228.2 19.9 %all-to-all-start.5 = ((bf16[64,8,768]{2,1,0:T(8,128)(2,1)}), bf16[64,8,768]{2,1,0:T(8,128)(2,1)S(1)}, u32[]{:S(2)}, u32[]{:S(2)}) async-start(bf16[64,8,768]{2,1,0:T(8,128)(2,1)} %bitcast.108), calls=%async_computation.5 | async-start | bytes 1572864 | tf_op jit(solution)/shard_map/all_to_all | solution.py:663
  232.9 61.0 %reduce-scatter.2.cloned.1.call-start = ((), (), s32[]{:S(2)}) async-start(), calls=%async_computation.9 | async-start | bytes 3276800 | tf_op jit(solution)/shard_map/reduce_scatter | solution.py:787
  248.2 0.9 copy-start.3
  249.1 13.0 %copy-start.13 = (bf16[2,50,768]{2,1,0:T(8,128)(2,1)S(1)}, bf16[2,50,768]{2,1,0:T(8,128)(2,1)}, u32[]{:S(2)}) copy-start(bf16[2,50,768]{2,1,0:T(8,128)(2,1)} %get-tuple-element.107) | copy-start | bytes 460804
  257.4 18.4 %all-to-all-start.6 = ((bf16[64,8,768]{2,1,0:T(8,128)(2,1)}), bf16[64,8,768]{2,1,0:T(8,128)(2,1)S(1)}, u32[]{:S(2)}, u32[]{:S(2)}) async-start(bf16[64,8,768]{2,1,0:T(8,128)(2,1)} %bitcast.109), calls=%async_computation.6 | async-start | bytes 1572864 | tf_op jit(solution)/shard_map/all_to_all | solution.py:663
  262.1 9.0 %collective-permute-start.7 = (bf16[2,50,768]{2,1,0:T(8,128)(2,1)S(1)}, bf16[2,50,768]{2,1,0:T(8,128)(2,1)S(1)}, u32[]{:S(2)}, u32[]{:S(2)}) collective-permute-start(bf16[2,50,768]{2,1,0:T(8,128)(2,1)S(1)} %copy-done.13), channel_id=1, source_target_pairs={{0,64},{64,0},{1,65},{65,1},{2,66},{66,2},{3,67},{67,3},{4,68},{68... | collective-permute-start | bytes 460808 | tf_op jit(solution)/shard_map/ppermute | solution.py:658
  275.8 0.9 copy-start.5
  289.6 9.0 %collective-permute-start.8 = (bf16[64,160,128]{2,1,0:T(8,128)(2,1)}, bf16[64,160,128]{2,1,0:T(8,128)(2,1)S(1)}, u32[]{:S(2)}, u32[]{:S(2)}) collective-permute-start(bf16[64,160,128]{2,1,0:T(8,128)(2,1)} %get-tuple-element.121), channel_id=1, source_target_pairs={{0,64},{64,0},{1,65},{65,1},{2,66},{66,2},{3,67},{67,3},{4,68},{68... | collective-permute-start | bytes 7864328 | tf_op jit(solution)/shard_map/ppermute | solution.py:658
  295.6 7.4 %collective-permute-start.10 = (bf16[4,160,128]{2,1,0:T(8,128)(2,1)}, bf16[4,160,128]{2,1,0:T(8,128)(2,1)S(1)}, u32[]{:S(2)}, u32[]{:S(2)}) collective-permute-start(bf16[4,160,128]{2,1,0:T(8,128)(2,1)} %get-tuple-element.150), channel_id=1, source_target_pairs={{0,8},{1,9},{2,10},{3,11},{4,12},{5,13},{6,14},{7,15},{8,0},{9,1},... | collective-permute-start | bytes 491528 | tf_op jit(solution)/shard_map/ppermute | solution.py:691
  297.1 8.5 %collective-permute-start.11 = (bf16[4,160,128]{2,1,0:T(8,128)(2,1)S(1)}, bf16[4,160,128]{2,1,0:T(8,128)(2,1)S(1)}, u32[]{:S(2)}, u32[]{:S(2)}) collective-permute-start(bf16[4,160,128]{2,1,0:T(8,128)(2,1)S(1)} %get-tuple-element.149), channel_id=1, source_target_pairs={{0,12},{1,13},{2,14},{3,15},{4,0},{5,1},{6,2},{7,3},{8,4},{9,5},{1... | collective-permute-start | bytes 491528 | tf_op jit(solution)/shard_map/ppermute | solution.py:691
  298.2 8.8 %collective-permute-start.9 = (bf16[4,160,128]{2,1,0:T(8,128)(2,1)S(1)}, bf16[4,160,128]{2,1,0:T(8,128)(2,1)}, u32[]{:S(2)}, u32[]{:S(2)}) collective-permute-start(bf16[4,160,128]{2,1,0:T(8,128)(2,1)S(1)} %get-tuple-element.148), channel_id=1, source_target_pairs={{0,4},{1,5},{2,6},{3,7},{4,8},{5,9},{6,10},{7,11},{8,12},{9,13},{1... | collective-permute-start | bytes 491528 | tf_op jit(solution)/shard_map/ppermute | solution.py:691
  308.1 18.5 %copy-start.11 = (bf16[2,50,768]{2,1,0:T(8,128)(2,1)S(1)}, bf16[2,50,768]{2,1,0:T(8,128)(2,1)}, u32[]{:S(2)}) copy-start(bf16[2,50,768]{2,1,0:T(8,128)(2,1)} %get-tuple-element.96) | copy-start | bytes 460804
  308.1 39.2 %all-to-all-start.7 = ((bf16[64,160,128]{2,1,0:T(8,128)(2,1)}), bf16[64,160,128]{2,1,0:T(8,128)(2,1)S(1)}, u32[]{:S(2)}, u32[]{:S(2)}) async-start(bf16[64,160,128]{2,1,0:T(8,128)(2,1)} %add.98), calls=%async_computation.8 | async-start | bytes 5242880 | tf_op jit(solution)/shard_map/all_to_all | solution.py:679
  314.0 13.6 %collective-permute-start.13 = (bf16[768,1536]{1,0:T(8,128)(2,1)}, bf16[768,1536]{1,0:T(8,128)(2,1)}, u32[]{:S(2)}, u32[]{:S(2)}) collective-permute-start(bf16[768,1536]{1,0:T(8,128)(2,1)} %get-tuple-element.125.refs_2_), channel_id=1, source_target_pairs={{0,64},{1,65},{2,66},{3,67},{4,68},{5,69},{6,70},{7,71},{8,72},{9,... | collective-permute-start | bytes 7077896 | tf_op jit(solution)/shard_map/ppermute | solution.py:796
  315.3 12.3 %collective-permute-start.15 = (bf16[1536,768]{1,0:T(8,128)(2,1)}, bf16[1536,768]{1,0:T(8,128)(2,1)}, u32[]{:S(2)}, u32[]{:S(2)}) collective-permute-start(bf16[1536,768]{1,0:T(8,128)(2,1)} %get-tuple-element.127.refs_6_), channel_id=1, source_target_pairs={{0,64},{1,65},{2,66},{3,67},{4,68},{5,69},{6,70},{7,71},{8,72},{9,... | collective-permute-start | bytes 7077896 | tf_op jit(solution)/shard_map/ppermute | solution.py:797
  316.6 11.0 %collective-permute-start.12 = (bf16[768,1536]{1,0:T(8,128)(2,1)}, bf16[768,1536]{1,0:T(8,128)(2,1)}, u32[]{:S(2)}, u32[]{:S(2)}) collective-permute-start(bf16[768,1536]{1,0:T(8,128)(2,1)} %get-tuple-element.124.refs_0_), channel_id=1, source_target_pairs={{64,0},{65,1},{66,2},{67,3},{68,4},{69,5},{70,6},{71,7},{72,8},{73... | collective-permute-start | bytes 7077896 | tf_op jit(solution)/shard_map/ppermute | solution.py:798
  323.9 6.4 %collective-permute-start.14 = (bf16[1536,768]{1,0:T(8,128)(2,1)}, bf16[1536,768]{1,0:T(8,128)(2,1)}, u32[]{:S(2)}, u32[]{:S(2)}) collective-permute-start(bf16[1536,768]{1,0:T(8,128)(2,1)} %get-tuple-element.126.refs_4_), channel_id=1, source_target_pairs={{64,0},{65,1},{66,2},{67,3},{68,4},{69,5},{70,6},{71,7},{72,8},{73... | collective-permute-start | bytes 7077896 | tf_op jit(solution)/shard_map/ppermute | solution.py:799
  326.6 18.1 %collective-permute-start.16 = (f32[2,50,768]{2,1,0:T(8,128)}, f32[2,50,768]{2,1,0:T(8,128)S(1)}, u32[]{:S(2)}, u32[]{:S(2)}) collective-permute-start(f32[2,50,768]{2,1,0:T(8,128)} %get-tuple-element.130), channel_id=1, source_target_pairs={{0,64},{64,0},{1,65},{65,1},{2,66},{66,2},{3,67},{67,3},{4,68},{68... | collective-permute-start | bytes 921608 | tf_op jit(solution)/shard_map/ppermute | solution.py:658
  339.5 12.0 %copy-start.9 = (f32[2,50,768]{2,1,0:T(8,128)S(1)}, f32[2,50,768]{2,1,0:T(8,128)}, u32[]{:S(2)}) copy-start(f32[2,50,768]{2,1,0:T(8,128)} %get-tuple-element.119) | copy-start | bytes 921604
  340.1 8.5 %collective-permute-start.17 = (bf16[160,128]{1,0:T(8,128)(2,1)}, bf16[160,128]{1,0:T(8,128)(2,1)S(1)}, u32[]{:S(2)}, u32[]{:S(2)}) collective-permute-start(bf16[160,128]{1,0:T(8,128)(2,1)} %get-tuple-element.155), channel_id=1, source_target_pairs={{0,1},{1,2},{2,3},{3,0},{4,5},{5,6},{6,7},{7,4},{8,9},{9,10},{10,1... | collective-permute-start | bytes 122888 | tf_op jit(solution)/shard_map/ppermute | solution.py:691
  341.1 8.0 %collective-permute-start.18 = (bf16[160,128]{1,0:T(8,128)(2,1)}, bf16[160,128]{1,0:T(8,128)(2,1)S(1)}, u32[]{:S(2)}, u32[]{:S(2)}) collective-permute-start(bf16[160,128]{1,0:T(8,128)(2,1)} %get-tuple-element.157), channel_id=1, source_target_pairs={{0,2},{1,3},{2,0},{3,1},{4,6},{5,7},{6,4},{7,5},{8,10},{9,11},{10,... | collective-permute-start | bytes 122888 | tf_op jit(solution)/shard_map/ppermute | solution.py:691
  343.5 5.6 %collective-permute-start.19 = (bf16[160,128]{1,0:T(8,128)(2,1)}, bf16[160,128]{1,0:T(8,128)(2,1)}, u32[]{:S(2)}, u32[]{:S(2)}) collective-permute-start(bf16[160,128]{1,0:T(8,128)(2,1)} %get-tuple-element.156), channel_id=1, source_target_pairs={{0,3},{1,0},{2,1},{3,2},{4,7},{5,4},{6,5},{7,6},{8,11},{9,8},{10,9... | collective-permute-start | bytes 122888 | tf_op jit(solution)/shard_map/ppermute | solution.py:691
  349.9 2.8 collective-permute-start.20
Sparse Core Ops, SparseCore 0:
  31.0 77.5 all-gather.2
  248.3 39.1 reduce-scatter.1
